TPU v7x, 32 devices: a whole 2x2x4 slice. The times are simulated.
32 devices in a mesh: groups: 2 (over x), tile: 16 (over z, y, core).
Axes of the slice: x: 2, y: 2, z: 4, core: 2. Of those that a mesh axis runs over, the one named last changes fastest.
Arguments:
- pair_tiles: bfloat16 [32, 64, 64, 128], P(('groups', 'tile')), parts along dimension 0, may hold values from -6 to 6
- cotangent: bfloat16 [32, 64, 64, 128], P(('groups', 'tile')), parts along dimension 0, may hold values from -6 to 6
- w_pair: bfloat16 [2, 128, 512], replicated, may hold values from -0.5 to 0.5
- w_gate: bfloat16 [2, 128, 128], replicated, may hold values from -0.5 to 0.5
- w_out: bfloat16 [2, 128, 128], replicated, may hold values from -0.5 to 0.5
- tile_lists: int32 [2, 32, 2, 2], P(None, 'groups'), parts along dimension 1, may hold values from 0 to 15
- list_counts: int32 [2, 32], P(None, 'groups'), parts along dimension 1, may hold values from 1 to 2
Outputs:
- new_pair: bfloat16 [32, 64, 64, 128], P(('groups', 'tile')), parts along dimension 0
- d_pair: bfloat16 [32, 64, 64, 128], P(('groups', 'tile')), parts along dimension 0
- grad_pair: float32 [4, 128, 512], P('groups', 'tile'), parts along dimension 0
- grad_gate: float32 [4, 128, 128], P('groups', 'tile'), parts along dimension 0
- grad_out: float32 [4, 128, 128], P('groups', 'tile'), parts along dimension 0
There are 2 independent parts, one for each index of `groups`. A program takes and returns all parts, laid end to end along the dimension named above; an argument that names none is the same for every part. Nothing has to cross between parts.
Inputs may be any that keep to these rules, and one draw needn't show every extreme that they name: `tile_lists`: each slot names two kept tiles by their index in the tile order; slots from list_counts on are unused.
All inputs are finite; a program needn't handle non-finite values.
Results may differ from a plain program's by a relative error of at most 0.015.
Values may be sent and summed in bfloat16 or wider, within the bound.
A program may use at most 192 MiB of HBM per device.

v0:
```python
import math

import jax
import jax.numpy as jnp
from jax import lax
from jax.sharding import PartitionSpec as P

EPS = 1e-05


def mixed_product(pattern, one_side, other_side):
    return jnp.einsum(pattern, one_side, other_side, preferred_element_type=jnp.float32)


def normalize(values, axis_index):
    center = jnp.mean(values, axis=axis_index, keepdims=True)
    shifted = values - center
    spread = jnp.mean(shifted * shifted, axis=axis_index, keepdims=True)
    factor = lax.rsqrt(spread + EPS)
    return (shifted * factor, factor)


def norm_back(upstream, normed, factor, axis_index):
    first_mean = jnp.mean(upstream, axis=axis_index, keepdims=True)
    cross_mean = jnp.mean(upstream * normed, axis=axis_index, keepdims=True)
    return factor * (upstream - first_mean - normed * cross_mean)


def project_in(pair_tiles, w_pair, w_gate):
    normed, in_factor = normalize(pair_tiles.astype(jnp.float32), 3)
    normed_low = normed.astype(jnp.bfloat16)
    projected = mixed_product("tijd,de->teij", normed_low, w_pair)
    channels = w_gate.shape[0]
    left_side = (
        projected[:, :channels] * jax.nn.sigmoid(projected[:, channels : 2 * channels])
    ).astype(jnp.bfloat16)
    right_side = (
        projected[:, 2 * channels : 3 * channels] * jax.nn.sigmoid(projected[:, 3 * channels :])
    ).astype(jnp.bfloat16)
    out_gate = jax.nn.sigmoid(mixed_product("tijd,de->tije", normed_low, w_gate))
    return (left_side, right_side, (normed, in_factor, normed_low, out_gate))


def project_out(pair_tiles, product, out_gate, w_out):
    normed, out_factor = normalize(product.astype(jnp.float32), 1)
    normed_low = normed.astype(jnp.bfloat16)
    update = mixed_product("tcij,ce->tije", normed_low, w_out)
    new_pair = (pair_tiles.astype(jnp.float32) + out_gate * update).astype(jnp.bfloat16)
    return (new_pair, (normed, out_factor, normed_low, update))


def triangle(left_chan, right_chan, slot_lists, amounts, incoming):
    pattern = "tcki,tckj->tcij" if incoming else "tcik,tcjk->tcij"

    def accumulate(column, summed):
        alive_mask = (column < amounts).astype(left_chan.dtype)[:, None, None, None]
        left_live = jnp.take(left_chan, slot_lists[:, column, 0], axis=0) * alive_mask
        right_rows = jnp.take(right_chan, slot_lists[:, column, 1], axis=0)
        return summed + mixed_product(pattern, left_live, right_rows)

    initial = jnp.zeros(left_chan.shape, jnp.float32)
    summed = lax.fori_loop(0, slot_lists.shape[1], accumulate, initial)
    return summed.astype(jnp.bfloat16)


def triangle_back(left_chan, right_chan, slot_lists, amounts, incoming, upstream):
    left_form = "tckj,tcij->tcki" if incoming else "tcjk,tcij->tcik"
    right_form = "tcki,tcij->tckj" if incoming else "tcik,tcij->tcjk"

    def accumulate(column, totals):
        left_index = slot_lists[:, column, 0]
        right_index = slot_lists[:, column, 1]
        alive_mask = (column < amounts).astype(left_chan.dtype)[:, None, None, None]
        left_live = jnp.take(left_chan, left_index, axis=0) * alive_mask
        right_live = jnp.take(right_chan, right_index, axis=0) * alive_mask
        left_grad = mixed_product(left_form, right_live, upstream)
        right_grad = mixed_product(right_form, left_live, upstream)
        return (totals[0].at[left_index].add(left_grad), totals[1].at[right_index].add(right_grad))

    initial = jnp.zeros(left_chan.shape, jnp.float32)
    left_total, right_total = lax.fori_loop(0, slot_lists.shape[1], accumulate, (initial, initial))
    return (left_total.astype(jnp.bfloat16), right_total.astype(jnp.bfloat16))


def back_out(upstream, out_saved, out_gate, w_out):
    normed, out_factor, normed_low, update = out_saved
    grad_update = (upstream * out_gate).astype(jnp.bfloat16)
    grad_logit = (upstream * update * out_gate * (1.0 - out_gate)).astype(jnp.bfloat16)
    grad_wout = mixed_product("tcij,tije->ce", normed_low, grad_update)
    grad_normed = mixed_product("tije,ce->tcij", grad_update, w_out)
    grad_product = norm_back(grad_normed, normed, out_factor, 1).astype(jnp.bfloat16)
    return (grad_product, grad_logit, grad_wout)


def back_in(residual_grad, grad_left, grad_right, grad_logit, in_saved, w_pair, w_gate):
    normed, in_factor, normed_low, out_gate = in_saved
    channels = w_gate.shape[0]
    projected = mixed_product("tijd,de->teij", normed_low, w_pair)
    left_val = projected[:, :channels]
    left_sig = jax.nn.sigmoid(projected[:, channels : 2 * channels])
    right_val = projected[:, 2 * channels : 3 * channels]
    right_sig = jax.nn.sigmoid(projected[:, 3 * channels :])
    left_flow = grad_left.astype(jnp.float32)
    right_flow = grad_right.astype(jnp.float32)
    grad_proj = jnp.concatenate(
        [
            left_flow * left_sig,
            left_flow * left_val * left_sig * (1.0 - left_sig),
            right_flow * right_sig,
            right_flow * right_val * right_sig * (1.0 - right_sig),
        ],
        axis=1,
    ).astype(jnp.bfloat16)
    grad_wpair = mixed_product("tijd,teij->de", normed_low, grad_proj)
    grad_wgate = mixed_product("tijd,tije->de", normed_low, grad_logit)
    grad_normed = mixed_product("teij,de->tijd", grad_proj, w_pair) + mixed_product(
        "tije,de->tijd", grad_logit, w_gate
    )
    return (residual_grad + norm_back(grad_normed, normed, in_factor, 3), grad_wpair, grad_wgate)


def forward_module(pair_tiles, w_pair, w_gate, w_out, slot_lists, amounts, incoming):
    left_side, right_side, in_saved = project_in(pair_tiles, w_pair, w_gate)
    left_chan, right_chan = (
        lax.all_to_all(left_side, "tile", split_axis=1, concat_axis=0, tiled=True),
        lax.all_to_all(right_side, "tile", split_axis=1, concat_axis=0, tiled=True),
    )
    product_chan = triangle(left_chan, right_chan, slot_lists, amounts, incoming)
    product = lax.all_to_all(product_chan, "tile", split_axis=0, concat_axis=1, tiled=True)
    new_pair, out_saved = project_out(pair_tiles, product, in_saved[3], w_out)
    return (new_pair, (left_chan, right_chan, in_saved, out_saved))


def backward_module(upstream, states, w_pair, w_gate, w_out, slot_lists, amounts, incoming):
    left_chan, right_chan, in_saved, out_saved = states
    grad_product, grad_logit, grad_wout = back_out(upstream, out_saved, in_saved[3], w_out)
    grad_chan = lax.all_to_all(grad_product, "tile", split_axis=1, concat_axis=0, tiled=True)
    grad_lchan, grad_rchan = triangle_back(
        left_chan, right_chan, slot_lists, amounts, incoming, grad_chan
    )
    grad_left, grad_right = (
        lax.all_to_all(grad_lchan, "tile", split_axis=0, concat_axis=1, tiled=True),
        lax.all_to_all(grad_rchan, "tile", split_axis=0, concat_axis=1, tiled=True),
    )
    grad_input, grad_wpair, grad_wgate = back_in(
        upstream, grad_left, grad_right, grad_logit, in_saved, w_pair, w_gate
    )
    return (grad_input, (grad_wpair, grad_wgate, grad_wout))


def local(pair_tiles, cotangent, w_pair, w_gate, w_out, tile_lists, list_counts):
    first_pair, first_saved = forward_module(
        pair_tiles, w_pair[0], w_gate[0], w_out[0], tile_lists[0], list_counts[0], False
    )
    new_pair, second_saved = forward_module(
        first_pair, w_pair[1], w_gate[1], w_out[1], tile_lists[1], list_counts[1], True
    )
    kept_states = (first_saved, second_saved)
    upstream = cotangent.astype(jnp.float32)
    collected = [None, None]
    for layer_index in (1, 0):
        states = kept_states[layer_index]
        upstream, weight_grads = backward_module(
            upstream,
            states,
            w_pair[layer_index],
            w_gate[layer_index],
            w_out[layer_index],
            tile_lists[layer_index],
            list_counts[layer_index],
            layer_index == 1,
        )
        collected[layer_index] = weight_grads
    pair_grad = jnp.stack([collected[0][0], collected[1][0]])
    gate_grad = jnp.stack([collected[0][1], collected[1][1]])
    out_grad = jnp.stack([collected[0][2], collected[1][2]])
    pair_grad, gate_grad, out_grad = (
        lax.psum_scatter(pair_grad, "tile", scatter_dimension=1, tiled=True),
        lax.psum_scatter(gate_grad, "tile", scatter_dimension=1, tiled=True),
        lax.psum_scatter(out_grad, "tile", scatter_dimension=1, tiled=True),
    )
    cell_count = tile_lists.shape[1] * pair_tiles.shape[1] * pair_tiles.shape[2]
    cell_scale = 1.0 / math.sqrt(cell_count)
    return (
        new_pair,
        upstream.astype(jnp.bfloat16),
        pair_grad * cell_scale,
        gate_grad * cell_scale,
        out_grad * cell_scale,
    )


def solution(mesh):
    in_specs = (
        P(("groups", "tile"), None, None, None),
        P(("groups", "tile"), None, None, None),
        P(),
        P(),
        P(),
        P(None, "groups", None, None),
        P(None, "groups"),
    )
    out_specs = (
        P(("groups", "tile"), None, None, None),
        P(("groups", "tile"), None, None, None),
        P("groups", "tile", None),
        P("groups", "tile", None),
        P("groups", "tile", None),
    )
    return jax.shard_map(local, mesh=mesh, in_specs=in_specs, out_specs=out_specs, check_vma=False)
```

profile of v0, /device:TPU:0, one launch (start us, length us, event | category | flops | bytes accessed | tf_op | source)
XLA Modules:
  0.0 935.6 jit_solution(9747798103146039430)
XLA Ops:
  22.7 7.4 all-to-all-start
  35.4 17.7 %all-to-all-done = bf16[16,2,16384]{2,1,0:T(2,128)(2,1)} async-done(((bf16[16,2,16384]{2,1,0:T(2,128)(2,1)}), bf16[16,2,16384]{2,1,0:T(2,128)(2,1)}, u32[]{:S(2)}, u32[]{:S(2)}) %all-to-all-start) | async-done | bytes 1048608 | tf_op jit(solution)/shard_map/all_to_all | solution.py:125
  53.1 7.0 all-to-all-start.1
  64.0 19.1 %all-to-all-done.1 = bf16[16,2,16384]{2,1,0:T(2,128)(2,1)S(1)} async-done(((bf16[16,2,16384]{2,1,0:T(2,128)(2,1)}), bf16[16,2,16384]{2,1,0:T(2,128)(2,1)S(1)}, u32[]{:S(2)}, u32[]{:S(2)}) %all-to-all-start.1) | async-done | bytes 1048608 | tf_op jit(solution)/shard_map/all_to_all | solution.py:126
  85.4 24.1 %while.60 = (s32[]{:T(128)}, f32[16,8,64,64]{3,2,1,0:T(8,128)}, s32[16,2,2]{0,2,1:T(2,128)S(1)}, bf16[16,8,64,64]{3,2,1,0:T(8,128)(2,1)S(1)}, s32[16]{0:T(128)S(...) while((s32[]{:T(128)}, f32[16,8,64,64]{3,2,1,0:T(8,128)}, ...), condition=%wide.region_3.5_spmd.clone, body=%wide.region_2.4_spmd.clone.sunk | while | flops 69732576 | bytes 10495775 | solution.py:62
  91.3 5.6 select_add_fusion.4
  102.7 6.8 select_add_fusion.4
  118.2 31.8 %all_to_all.126 = bf16[16,2,16384]{2,1,0:T(2,128)(2,1)} all-to-all(bf16[16,2,16384]{2,1,0:T(2,128)(2,1)S(1)} %reshape.743), channel_id=1, replica_groups=mesh['groups'=2,'tile'=16] {'tile'}, dimensions={0} | all-to-all | bytes 2097152 | tf_op jit(solution)/shard_map/all_to_all | solution.py:129
  178.5 5.3 all-to-all-start.3
  190.0 16.8 %all-to-all-done.3 = bf16[16,2,16384]{2,1,0:T(2,128)(2,1)} async-done(((bf16[16,2,16384]{2,1,0:T(2,128)(2,1)}), bf16[16,2,16384]{2,1,0:T(2,128)(2,1)}, u32[]{:S(2)}, u32[]{:S(2)}) %all-to-all-start.3) | async-done | bytes 1048608 | tf_op jit(solution)/shard_map/all_to_all | solution.py:125
  206.7 6.9 all-to-all-start.4
  217.4 19.2 %all-to-all-done.4 = bf16[16,2,16384]{2,1,0:T(2,128)(2,1)} async-done(((bf16[16,2,16384]{2,1,0:T(2,128)(2,1)}), bf16[16,2,16384]{2,1,0:T(2,128)(2,1)}, u32[]{:S(2)}, u32[]{:S(2)}) %all-to-all-start.4) | async-done | bytes 1048608 | tf_op jit(solution)/shard_map/all_to_all | solution.py:126
  241.3 23.7 %while.61 = (s32[]{:T(128)}, f32[16,8,64,64]{3,2,1,0:T(8,128)}, s32[16,2,2]{0,2,1:T(2,128)S(1)}, bf16[16,8,64,64]{3,2,1,0:T(8,128)(2,1)S(1)}, s32[16]{0:T(128)S(...) while((s32[]{:T(128)}, f32[16,8,64,64]{3,2,1,0:T(8,128)}, ...), condition=%wide.region_9.11_spmd.clone, body=%wide.region_8.10_spmd.clone.sunk | while | flops 69732576 | bytes 10495775 | solution.py:62
  247.3 5.3 select_add_fusion.5
  258.5 6.5 select_add_fusion.5
  274.5 7.4 all-to-all-start.5
  284.5 20.4 %all-to-all-done.5 = bf16[16,2,16384]{2,1,0:T(2,128)(2,1)} async-done(((bf16[16,2,16384]{2,1,0:T(2,128)(2,1)}), bf16[16,2,16384]{2,1,0:T(2,128)(2,1)}, u32[]{:S(2)}, u32[]{:S(2)}) %all-to-all-start.5) | async-done | bytes 1048608 | tf_op jit(solution)/shard_map/all_to_all | solution.py:129
  327.3 7.1 all-to-all-start.6
  334.4 23.0 %all-to-all-done.6 = bf16[16,2,16384]{2,1,0:T(2,128)(2,1)} async-done(((bf16[16,2,16384]{2,1,0:T(2,128)(2,1)}), bf16[16,2,16384]{2,1,0:T(2,128)(2,1)}, u32[]{:S(2)}, u32[]{:S(2)}) %all-to-all-start.6) | async-done | bytes 1048608 | tf_op jit(solution)/shard_map/all_to_all | solution.py:137
  366.3 71.2 %while.58 = (s32[]{:T(128)}, f32[16,8,64,64]{3,2,1,0:T(8,128)}, f32[16,8,64,64]{3,2,1,0:T(8,128)}, s32[16,2,2]{0,2,1:T(2,128)S(1)}, bf16[16,8,64,64]{3,2,1,0:T(8...) while((s32[]{:T(128)}, f32[16,8,64,64]{3,2,1,0:T(8,128)}, ...), condition=%wide.region_17.0_spmd, body=%wide.region_14.18_spmd.sunk | while | flops 137365824 | bytes 25176256 | solution.py:81
  374.4 9.5 %scatter_fusion.1 = f32[16,8,64,64]{3,2,1,0:T(8,128)} fusion(f32[16,8,64,64]{3,2,1,0:T(8,128)} %get-tuple-element.986, s32[16]{0:T(128)S(1)} %get-tuple-element.887, f32[16,8,64,64]{3,2,1,0:T(8,128)} %fusion.174), kind=kCustom, calls=%fused_computation.9.clone.1 | custom fusion | flops 524288 | bytes 6291520 | tf_op jit(solution)/shard_map/while/body/eval_jaxpr/scatter-add | solution.py:78
  392.5 9.5 %scatter_fusion = f32[16,8,64,64]{3,2,1,0:T(8,128)} fusion(f32[16,8,64,64]{3,2,1,0:T(8,128)} %get-tuple-element.985, s32[16]{0:T(128)S(1)} %get-tuple-element.883, f32[16,8,64,64]{3,2,1,0:T(8,128)} %fusion.173), kind=kCustom, calls=%fused_computation.8.clone.1 | custom fusion | flops 524288 | bytes 6291520 | tf_op jit(solution)/shard_map/while/body/eval_jaxpr/scatter-add | solution.py:78
  410.2 9.4 %scatter_fusion.1 = f32[16,8,64,64]{3,2,1,0:T(8,128)} fusion(f32[16,8,64,64]{3,2,1,0:T(8,128)} %get-tuple-element.986, s32[16]{0:T(128)S(1)} %get-tuple-element.887, f32[16,8,64,64]{3,2,1,0:T(8,128)} %fusion.174), kind=kCustom, calls=%fused_computation.9.clone.1 | custom fusion | flops 524288 | bytes 6291520 | tf_op jit(solution)/shard_map/while/body/eval_jaxpr/scatter-add | solution.py:78
  428.2 9.3 scatter_fusion
  442.4 6.9 all-to-all-start.7
  458.2 14.1 %all-to-all-done.7 = bf16[16,2,16384]{2,1,0:T(2,128)(2,1)} async-done(((bf16[16,2,16384]{2,1,0:T(2,128)(2,1)}), bf16[16,2,16384]{2,1,0:T(2,128)(2,1)}, u32[]{:S(2)}, u32[]{:S(2)}) %all-to-all-start.7) | async-done | bytes 1048608 | tf_op jit(solution)/shard_map/all_to_all | solution.py:142
  472.4 7.1 all-to-all-start.8
  518.8 5.7 fusion.83
  528.9 5.5 fusion.94
  546.3 31.2 %all_to_all.127 = bf16[16,2,16384]{2,1,0:T(2,128)(2,1)} all-to-all(bf16[16,2,16384]{2,1,0:T(2,128)(2,1)} %reshape.757), channel_id=1, replica_groups=mesh['groups'=2,'tile'=16] {'tile'}, dimensions={0} | all-to-all | bytes 2097152 | tf_op jit(solution)/shard_map/all_to_all | solution.py:137
  586.3 94.9 %while.59 = (s32[]{:T(128)}, f32[16,8,64,64]{3,2,1,0:T(8,128)}, f32[16,8,64,64]{3,2,1,0:T(8,128)}, s32[16,2,2]{0,2,1:T(2,128)S(1)}, bf16[16,8,64,64]{3,2,1,0:T(8...) while((s32[]{:T(128)}, f32[16,8,64,64]{3,2,1,0:T(8,128)}, ...), condition=%wide.region_25.0_spmd, body=%wide.region_22.26_spmd.sunk | while | flops 137365824 | bytes 33564864 | solution.py:81
  594.7 5.4 copy.93
  600.0 9.6 %scatter_fusion.3 = f32[16,8,64,64]{3,2,1,0:T(8,128)} fusion(f32[16,8,64,64]{3,2,1,0:T(8,128)} %get-tuple-element.1013, s32[16]{0:T(128)S(1)} %get-tuple-element.902, f32[16,8,64,64]{3,2,1,0:T(8,128)} %copy.93), kind=kCustom, calls=%fused_computation.11.clone.1 | custom fusion | flops 524288 | bytes 6291520 | tf_op jit(solution)/shard_map/while/body/eval_jaxpr/scatter-add | solution.py:78
  613.4 5.6 convolution_bitcast_fusion.12
  619.0 5.4 copy.92
  624.3 9.4 %scatter_fusion.2 = f32[16,8,64,64]{3,2,1,0:T(8,128)} fusion(f32[16,8,64,64]{3,2,1,0:T(8,128)} %get-tuple-element.1012, s32[16]{0:T(128)S(1)} %get-tuple-element.898, f32[16,8,64,64]{3,2,1,0:T(8,128)} %copy.92), kind=kCustom, calls=%fused_computation.10.clone.1 | custom fusion | flops 524288 | bytes 6291520 | tf_op jit(solution)/shard_map/while/body/eval_jaxpr/scatter-add | solution.py:78
  642.1 5.4 copy.93
  647.5 9.5 %scatter_fusion.3 = f32[16,8,64,64]{3,2,1,0:T(8,128)} fusion(f32[16,8,64,64]{3,2,1,0:T(8,128)} %get-tuple-element.1013, s32[16]{0:T(128)S(1)} %get-tuple-element.902, f32[16,8,64,64]{3,2,1,0:T(8,128)} %copy.93), kind=kCustom, calls=%fused_computation.11.clone.1 | custom fusion | flops 524288 | bytes 6291520 | tf_op jit(solution)/shard_map/while/body/eval_jaxpr/scatter-add | solution.py:78
  660.8 5.6 convolution_bitcast_fusion.12
  666.4 5.4 copy.92
  671.8 9.5 %scatter_fusion.2 = f32[16,8,64,64]{3,2,1,0:T(8,128)} fusion(f32[16,8,64,64]{3,2,1,0:T(8,128)} %get-tuple-element.1012, s32[16]{0:T(128)S(1)} %get-tuple-element.898, f32[16,8,64,64]{3,2,1,0:T(8,128)} %copy.92), kind=kCustom, calls=%fused_computation.10.clone.1 | custom fusion | flops 524288 | bytes 6291520 | tf_op jit(solution)/shard_map/while/body/eval_jaxpr/scatter-add | solution.py:78
  698.2 16.1 %all-to-all-done.10 = bf16[16,2,16384]{2,1,0:T(2,128)(2,1)} async-done(((bf16[16,2,16384]{2,1,0:T(2,128)(2,1)}), bf16[16,2,16384]{2,1,0:T(2,128)(2,1)}, u32[]{:S(2)}, u32[]{:S(2)}) %all-to-all-start.10) | async-done | bytes 1048608 | tf_op jit(solution)/shard_map/all_to_all | solution.py:142
  714.3 6.9 all-to-all-start.11
  732.8 45.5 %reduce-scatter.8.cloned.1.call-done = f32[2,8,128]{2,1,0:T(8,128)} async-done(((f32[2,128,128]{2,1,0:T(8,128)}), f32[2,8,128]{2,1,0:T(8,128)}) %reduce-scatter.8.cloned.1.call-update) | async-done | bytes 8208 | tf_op jit(solution)/shard_map/reduce_scatter | solution.py:180
  779.6 53.6 %reduce-scatter.6.cloned.1.call-done = f32[2,8,128]{2,1,0:T(8,128)} async-done(((f32[2,128,128]{2,1,0:T(8,128)}), f32[2,8,128]{2,1,0:T(8,128)}) %reduce-scatter.6.cloned.1.call-update) | async-done | bytes 8208 | tf_op jit(solution)/shard_map/reduce_scatter | solution.py:179
  861.5 5.8 fusion.87
  880.2 8.2 fusion.52
  888.4 39.1 %reduce-scatter.4.cloned.1.call-done = f32[2,8,512]{2,1,0:T(8,128)} async-done(((f32[2,128,512]{2,1,0:T(8,128)}), f32[2,8,512]{2,1,0:T(8,128)}) %reduce-scatter.4.cloned.1.call-update) | async-done | bytes 32784 | tf_op jit(solution)/shard_map/reduce_scatter | solution.py:178
  (283 shorter events, 353.1 us)
Async XLA Ops:
  7.2 4.4 copy-start.10
  7.2 4.4 copy-start.42
  9.1 152.0 %copy-start.36 = (f32[64,64]{1,0:T(8,128)}, f32[64,64]{1,0:T(8,128)S(1)}, u32[]{:S(2)}) copy-start(f32[64,64]{1,0:T(8,128)S(1)} %broadcast_multiply_fusion.12) | copy-start | bytes 49156
  11.5 149.6 %copy-start.38 = (f32[64,64]{1,0:T(8,128)}, f32[64,64]{1,0:T(8,128)S(1)}, u32[]{:S(2)}) copy-start(f32[64,64]{1,0:T(8,128)S(1)} %add_rsqrt_fusion.3) | copy-start | bytes 49156
  12.9 3.6 copy-start.3
  22.7 30.4 %all-to-all-start = ((bf16[16,2,16384]{2,1,0:T(2,128)(2,1)}), bf16[16,2,16384]{2,1,0:T(2,128)(2,1)}, u32[]{:S(2)}, u32[]{:S(2)}) async-start(bf16[16,2,16384]{2,1,0:T(2,128)(2,1)} %reshape.739), calls=%async_computation | async-start | bytes 2097152 | tf_op jit(solution)/shard_map/all_to_all | solution.py:125
  33.1 27.1 %copy-start.56 = (s32[2,16]{1,0:T(2,128)S(1)}, s32[2,16]{1,0:T(2,128)}, u32[]{:S(2)}) copy-start(s32[2,16]{1,0:T(2,128)} %param.23) | copy-start | bytes 388
  33.1 27.1 %copy-start.55 = (s32[2,16,2,2]{1,3,2,0:T(2,128)S(1)}, s32[2,16,2,2]{1,3,2,0:T(2,128)}, u32[]{:S(2)}) copy-start(s32[2,16,2,2]{1,3,2,0:T(2,128)} %param.22) | copy-start | bytes 1540
  53.1 30.0 %all-to-all-start.1 = ((bf16[16,2,16384]{2,1,0:T(2,128)(2,1)}), bf16[16,2,16384]{2,1,0:T(2,128)(2,1)S(1)}, u32[]{:S(2)}, u32[]{:S(2)}) async-start(bf16[16,2,16384]{2,1,0:T(2,128)(2,1)} %reshape.741), calls=%async_computation.1 | async-start | bytes 2097152 | tf_op jit(solution)/shard_map/all_to_all | solution.py:126
  109.5 4.8 copy-start
  109.5 4.8 copy-start.48
  109.5 4.8 copy-start.53
  154.3 3.0 copy-start.34
  157.3 3.4 copy-start.45
  160.7 5.0 copy-start.23
  162.3 3.4 copy-start.21
  168.3 3.9 copy-start.4
  178.5 28.3 %all-to-all-start.3 = ((bf16[16,2,16384]{2,1,0:T(2,128)(2,1)}), bf16[16,2,16384]{2,1,0:T(2,128)(2,1)}, u32[]{:S(2)}, u32[]{:S(2)}) async-start(bf16[16,2,16384]{2,1,0:T(2,128)(2,1)} %reshape.745), calls=%async_computation.3 | async-start | bytes 2097152 | tf_op jit(solution)/shard_map/all_to_all | solution.py:125
  206.7 29.9 %all-to-all-start.4 = ((bf16[16,2,16384]{2,1,0:T(2,128)(2,1)}), bf16[16,2,16384]{2,1,0:T(2,128)(2,1)}, u32[]{:S(2)}, u32[]{:S(2)}) async-start(bf16[16,2,16384]{2,1,0:T(2,128)(2,1)} %reshape.747), calls=%async_computation.4 | async-start | bytes 2097152 | tf_op jit(solution)/shard_map/all_to_all | solution.py:126
  265.0 4.8 copy-start.1
  269.8 12.1 %copy-start.51 = (bf16[2,128,128]{2,1,0:T(8,128)(2,1)S(1)}, bf16[2,128,128]{2,1,0:T(8,128)(2,1)}, u32[]{:S(2)}) copy-start(bf16[2,128,128]{2,1,0:T(8,128)(2,1)} %param.20) | copy-start | bytes 196612
  274.5 30.4 %all-to-all-start.5 = ((bf16[16,2,16384]{2,1,0:T(2,128)(2,1)}), bf16[16,2,16384]{2,1,0:T(2,128)(2,1)}, u32[]{:S(2)}, u32[]{:S(2)}) async-start(bf16[16,2,16384]{2,1,0:T(2,128)(2,1)} %reshape.749), calls=%async_computation.5 | async-start | bytes 2097152 | tf_op jit(solution)/shard_map/all_to_all | solution.py:129
  308.7 3.6 copy-start.7
  313.5 4.3 copy-start.17
  327.3 30.1 %all-to-all-start.6 = ((bf16[16,2,16384]{2,1,0:T(2,128)(2,1)}), bf16[16,2,16384]{2,1,0:T(2,128)(2,1)}, u32[]{:S(2)}, u32[]{:S(2)}) async-start(bf16[16,2,16384]{2,1,0:T(2,128)(2,1)} %reshape.751), calls=%async_computation.6 | async-start | bytes 2097152 | tf_op jit(solution)/shard_map/all_to_all | solution.py:137
  442.4 29.9 %all-to-all-start.7 = ((bf16[16,2,16384]{2,1,0:T(2,128)(2,1)}), bf16[16,2,16384]{2,1,0:T(2,128)(2,1)}, u32[]{:S(2)}, u32[]{:S(2)}) async-start(bf16[16,2,16384]{2,1,0:T(2,128)(2,1)} %reshape.755), calls=%async_computation.7 | async-start | bytes 2097152 | tf_op jit(solution)/shard_map/all_to_all | solution.py:142
  453.4 26.1 %copy-start.6 = (bf16[16,8,64,64]{3,2,1,0:T(8,128)(2,1)S(1)}, bf16[16,8,64,64]{3,2,1,0:T(8,128)(2,1)}, u32[]{:S(2)}) copy-start(bf16[16,8,64,64]{3,2,1,0:T(8,128)(2,1)} %copy-done.5) | copy-start | bytes 3145732
  472.4 35.2 %all-to-all-start.8 = ((bf16[16,2,16384]{2,1,0:T(2,128)(2,1)}), bf16[16,2,16384]{2,1,0:T(2,128)(2,1)}, u32[]{:S(2)}, u32[]{:S(2)}) async-start(bf16[16,2,16384]{2,1,0:T(2,128)(2,1)} %reshape.753), calls=%async_computation.8 | async-start | bytes 2097152 | tf_op jit(solution)/shard_map/all_to_all | solution.py:143
  486.5 3.4 copy-start.14
  489.9 4.1 copy-start.19
  513.7 5.0 copy-start.22
  518.8 5.7 copy-start.43
  528.3 6.2 copy-start.8
  528.9 5.5 copy-start.18
  528.9 5.5 copy-start.35
  528.9 5.5 copy-start.41
  686.1 5.2 copy-start.26
  686.2 6.8 copy-start.20
  686.2 28.2 %all-to-all-start.10 = ((bf16[16,2,16384]{2,1,0:T(2,128)(2,1)}), bf16[16,2,16384]{2,1,0:T(2,128)(2,1)}, u32[]{:S(2)}, u32[]{:S(2)}) async-start(bf16[16,2,16384]{2,1,0:T(2,128)(2,1)} %reshape.761), calls=%async_computation.10 | async-start | bytes 2097152 | tf_op jit(solution)/shard_map/all_to_all | solution.py:142
  698.2 23.3 %copy-start.24 = (bf16[128,64,64]{0,2,1:T(8,128)(2,1)S(1)}, bf16[128,64,64]{0,2,1:T(8,128)(2,1)}, u32[]{:S(2)}) copy-start(bf16[128,64,64]{0,2,1:T(8,128)(2,1)} %copy-done.23) | copy-start | bytes 3145732
  698.2 25.8 %copy-start.12 = (bf16[1,64,64,128]{3,2,1,0:T(8,128)(2,1)S(1)}, bf16[1,64,64,128]{3,2,1,0:T(8,128)(2,1)}, u32[]{:S(2)}) copy-start(bf16[1,64,64,128]{3,2,1,0:T(8,128)(2,1)} %param.17) | copy-start | bytes 3145732
  698.2 25.8 %copy-start.37 = (f32[64,64]{1,0:T(8,128)S(1)}, f32[64,64]{1,0:T(8,128)}, u32[]{:S(2)}) copy-start(f32[64,64]{1,0:T(8,128)} %copy-done.36) | copy-start | bytes 49156
  698.2 25.8 %copy-start.39 = (f32[64,64]{1,0:T(8,128)S(1)}, f32[64,64]{1,0:T(8,128)}, u32[]{:S(2)}) copy-start(f32[64,64]{1,0:T(8,128)} %copy-done.38) | copy-start | bytes 49156
  714.3 133.7 %all-to-all-start.11 = ((bf16[16,2,16384]{2,1,0:T(2,128)(2,1)}), bf16[16,2,16384]{2,1,0:T(2,128)(2,1)}, u32[]{:S(2)}, u32[]{:S(2)}) async-start(bf16[16,2,16384]{2,1,0:T(2,128)(2,1)} %reshape.759), calls=%async_computation.11 | async-start | bytes 2097152 | tf_op jit(solution)/shard_map/all_to_all | solution.py:143
  721.2 57.0 %reduce-scatter.8.cloned.1.call-start = ((), (), s32[]{:S(2)}) async-start(), calls=%async_computation.17 | async-start | bytes 139264 | tf_op jit(solution)/shard_map/reduce_scatter | solution.py:180
  723.2 4.3 copy-start.30
  723.9 109.2 %reduce-scatter.6.cloned.1.call-start = ((), (), s32[]{:S(2)}) async-start(), calls=%async_computation.16 | async-start | bytes 139264 | tf_op jit(solution)/shard_map/reduce_scatter | solution.py:179
  727.5 200.0 %reduce-scatter.4.cloned.1.call-start = ((), (), s32[]{:S(2)}) async-start(), calls=%async_computation.15 | async-start | bytes 557056 | tf_op jit(solution)/shard_map/reduce_scatter | solution.py:178
  (22 other events, 40.6 us)
Sparse Core Ops, SparseCore 0:
  725.4 52.7 reduce-scatter.7
  782.0 51.1 reduce-scatter.5
  872.6 54.7 reduce-scatter.3
where the time goes:
time: 946 us; the launch traced here: 936 us
  waiting for transfers between devices  285 us (30%)
  local copies, waits for them, and re-layouts  229 us (24%)
  other arithmetic  170 us (18%)
  matrix products  106 us (11%)
  starting transfers between devices  67.7 us (7%)
  blocking collectives  63.1 us (7%)
  between operations  14.9 us (2%)
    dot_general x30, matrix products, mixed_product(): jnp.einsum(pattern, one_side, other_side, preferred_element_type=jnp.floa...  106 us
    unnamed x138, local copies, waits for them, and re-layouts  88.3 us
    reduce_scatter x1, waiting for transfers between devices, local(): lax.psum_scatter(gate_grad, 'tile', scatter_dimension=1, tiled=True)  53.6 us
    reduce_scatter x1, waiting for transfers between devices, local(): lax.psum_scatter(out_grad, 'tile', scatter_dimension=1, tiled=True)  45.5 us
    reduce_scatter x1, waiting for transfers between devices, local(): lax.psum_scatter(pair_grad, 'tile', scatter_dimension=1, tiled=True)  39.1 us
    all_to_all x2, waiting for transfers between devices, forward_module(): lax.all_to_all(right_side, 'tile', split_axis=1, concat_axis=0, tiled=True)  38.3 us
    scatter-add x4, other arithmetic, accumulate(): totals[1].at[right_index].add(right_grad)  38.1 us
    scatter-add x4, other arithmetic, accumulate(): totals[0].at[left_index].add(left_grad)  37.7 us
  transfers between devices with their start and end apart: 13, of which 11 were waited for; matrix products, arithmetic and copies ran while one was open for 11% of the time, Pallas kernels for 0%

commit v1 on v0

v1 whole, which is shorter than its diff:
```python
import functools
import math

import jax
import jax.numpy as jnp
from jax import lax
from jax.experimental import pallas as pl
from jax.experimental.pallas import tpu as pltpu
from jax.sharding import PartitionSpec as P

EPS = 1e-05
CHUNK = 512
VMEM_BYTES = 40 * 1024 * 1024
F32, BF16 = jnp.float32, jnp.bfloat16


def dot(one, other, one_dim, other_dim):
    return lax.dot_general(one, other, (((one_dim,), (other_dim,)), ((), ())), preferred_element_type=F32)


def sigmoid(values):
    return 0.5 * jnp.tanh(0.5 * values) + 0.5


def normalize(values):
    shifted = values - jnp.mean(values, axis=0, keepdims=True)
    factor = lax.rsqrt(jnp.mean(shifted * shifted, axis=0, keepdims=True) + EPS)
    return shifted * factor, factor


def norm_back(upstream, normed, factor):
    first_mean = jnp.mean(upstream, axis=0, keepdims=True)
    cross_mean = jnp.mean(upstream * normed, axis=0, keepdims=True)
    return factor * (upstream - first_mean - normed * cross_mean)


def gated(normed_low, w_val, w_sig):
    return dot(w_val, normed_low, 1, 0), sigmoid(dot(w_sig, normed_low, 1, 0))


def project_in(pair, w_val, w_sig, lr_ref):
    normed_low = normalize(pair)[0].astype(BF16)
    value, sig = gated(normed_low, w_val[...], w_sig[...])
    lr_ref[...] = (value * sig).astype(BF16)


def out_parts(pair, prod_ref, w_gate, w_out):
    in_low = normalize(pair)[0].astype(BF16)
    gate = sigmoid(dot(w_gate[...], in_low, 0, 0))
    normed, factor = normalize(prod_ref[...].astype(F32))
    normed_low = normed.astype(BF16)
    update = dot(w_out[...], normed_low, 0, 0)
    return in_low, gate, normed, factor, normed_low, update


def accumulate(ref, value):
    @pl.when(pl.program_id(0) == 0)
    def _():
        ref[...] = jnp.zeros_like(ref)

    ref[...] += value


def back_out(upstream, parts, w_out, gprod_ref, glogit_ref, dgate_ref, dout_ref):
    in_low, gate, normed, factor, normed_low, update = parts
    grad_update = (upstream * gate).astype(BF16)
    grad_logit = (upstream * update * gate * (1.0 - gate)).astype(BF16)
    glogit_ref[...] = grad_logit
    accumulate(dout_ref, dot(normed_low, grad_update, 1, 1))
    accumulate(dgate_ref, dot(in_low, grad_logit, 1, 1))
    grad_normed = dot(w_out[...], grad_update, 1, 0)
    gprod_ref[...] = norm_back(grad_normed, normed, factor).astype(BF16)


def back_in(upstream, pair, glr_ref, glogit_ref, w_val, w_sig, w_gate, dpair_ref):
    normed, factor = normalize(pair)
    normed_low = normed.astype(BF16)
    value, sig = gated(normed_low, w_val[...], w_sig[...])
    flow = glr_ref[...].astype(F32)
    grad_val = flow * sig
    grad_sig = (grad_val * value * (1.0 - sig)).astype(BF16)
    grad_val = grad_val.astype(BF16)
    rows = grad_val.shape[0]
    accumulate(dpair_ref.at[:, :rows], dot(normed_low, grad_val, 1, 1))
    accumulate(dpair_ref.at[:, rows:], dot(normed_low, grad_sig, 1, 1))
    grad_normed = (
        dot(w_val[...], grad_val, 0, 0)
        + dot(w_sig[...], grad_sig, 0, 0)
        + dot(w_gate[...], glogit_ref[...], 1, 0)
    )
    return upstream + norm_back(grad_normed, normed, factor)


def turned(ref):
    return ref[...].astype(F32).T


def first_kernel(x_ref, wv, ws, lr_ref):
    project_in(turned(x_ref), wv, ws, lr_ref)


def middle_kernel(x_ref, prod_ref, wgate, wout, wv, ws, pair_ref, lr_ref):
    pair = turned(x_ref)
    _, gate, _, _, _, update = out_parts(pair, prod_ref, wgate, wout)
    low = (pair + gate * update).astype(BF16)
    pair_ref[...] = low
    project_in(low.astype(F32), wv, ws, lr_ref)


def top_kernel(pair_ref, prod_ref, cot_ref, wgate, wout, new_ref, gprod_ref, glogit_ref, dgate_ref, dout_ref):
    pair = pair_ref[...].astype(F32)
    parts = out_parts(pair, prod_ref, wgate, wout)
    new_ref[...] = (pair + parts[1] * parts[5]).T.astype(BF16)
    back_out(turned(cot_ref), parts, wout, gprod_ref, glogit_ref, dgate_ref, dout_ref)


def turn_kernel(
    pair_ref, cot_ref, glr_ref, glogit1_ref, x_ref, prod_ref, wv1, ws1, wgate1, wgate0, wout0,
    up_ref, gprod_ref, glogit_ref, dpair_ref, dgate_ref, dout_ref,
):
    upstream = back_in(
        turned(cot_ref), pair_ref[...].astype(F32), glr_ref, glogit1_ref, wv1, ws1, wgate1, dpair_ref
    )
    up_ref[...] = upstream
    parts = out_parts(turned(x_ref), prod_ref, wgate0, wout0)
    back_out(upstream, parts, wout0, gprod_ref, glogit_ref, dgate_ref, dout_ref)


def last_kernel(x_ref, up_ref, glr_ref, glogit_ref, wv, ws, wgate, dx_ref, dpair_ref):
    grad = back_in(up_ref[...], turned(x_ref), glr_ref, glogit_ref, wv, ws, wgate, dpair_ref)
    dx_ref[...] = grad.T.astype(BF16)


def cellwise(kernel, name, args, outs, cells):
    step = min(CHUNK, cells)

    def spec(kind, shape):
        if kind == "r":
            return pl.BlockSpec((step, shape[1]), lambda n: (n, 0))
        if kind == "c":
            return pl.BlockSpec((shape[0], step), lambda n: (0, n))
        return pl.BlockSpec(shape, lambda n: (0, 0))

    return pl.pallas_call(
        kernel,
        name=name,
        grid=(cells // step,),
        in_specs=[spec(kind, array.shape) for kind, array in args],
        out_specs=[spec(kind, shape) for kind, shape, _ in outs],
        out_shape=[jax.ShapeDtypeStruct(shape, kind) for _, shape, kind in outs],
        compiler_params=pltpu.CompilerParams(vmem_limit_bytes=VMEM_BYTES),
    )(*[array for _, array in args])


def triangle_kernel(incoming, tiles, kmax, chans, lists, counts, lr_ref, prod_ref):
    dim = 0 if incoming else 1

    def one(tile, _):
        def term(slot, chan):
            base = (tile * kmax + slot) * 2
            return dot(lr_ref[lists[base], chan], lr_ref[lists[base + 1], chans + chan], dim, dim)

        used = counts[tile]
        for chan in range(chans):
            total = term(0, chan)
            for slot in range(1, kmax):
                total = total + jnp.where(slot < used, term(slot, chan), 0.0)
            prod_ref[tile, chan] = total.astype(BF16)
        return 0

    lax.fori_loop(0, tiles, one, 0)


def triangle_back_kernel(incoming, tiles, kmax, chans, lists, counts, lr_ref, gprod_ref, glr_ref, total):
    total[...] = jnp.zeros_like(total)

    def one(tile, _):
        for slot in range(kmax):

            @pl.when(slot < counts[tile])
            def _():
                base = (tile * kmax + slot) * 2
                x, y = lists[base], lists[base + 1]
                for chan in range(chans):
                    grad = gprod_ref[tile, chan]
                    left, right = lr_ref[x, chan], lr_ref[y, chans + chan]
                    if incoming:
                        total[x, chan] += dot(right, grad, 1, 1)
                        total[y, chans + chan] += dot(left, grad, 1, 0)
                    else:
                        total[x, chan] += dot(grad, right, 1, 0)
                        total[y, chans + chan] += dot(grad, left, 0, 0)
        return 0

    lax.fori_loop(0, tiles, one, 0)

    def store(tile, _):
        glr_ref[tile] = total[tile].astype(BF16)
        return 0

    lax.fori_loop(0, tiles, store, 0)


def tile_call(kernel, name, scalars, arrays, out_shape, scratch):
    return pl.pallas_call(
        kernel,
        name=name,
        in_specs=[pl.BlockSpec(memory_space=pltpu.SMEM)] * len(scalars)
        + [pl.BlockSpec(memory_space=pltpu.VMEM)] * len(arrays),
        out_specs=pl.BlockSpec(memory_space=pltpu.VMEM),
        out_shape=jax.ShapeDtypeStruct(out_shape, BF16),
        scratch_shapes=scratch,
        compiler_params=pltpu.CompilerParams(vmem_limit_bytes=VMEM_BYTES),
    )(*scalars, *arrays)


def exchange(array):
    return lax.all_to_all(array, "tile", split_axis=0, concat_axis=0, tiled=True)


def local(devices, pair_tiles, cotangent, w_pair, w_gate, w_out, tile_lists, list_counts):
    owned, side, _, channels = pair_tiles.shape
    cells = owned * side * side
    tiles, kmax = tile_lists.shape[1], tile_lists.shape[2]
    chans = channels // devices
    x = pair_tiles.reshape(cells, channels)
    cot = cotangent.reshape(cells, channels)
    weights = w_pair.reshape(2, channels, 2, 2, devices, chans)
    weights = weights.transpose(0, 3, 4, 2, 5, 1).reshape(2, 2, 2 * channels, channels)
    wide = 2 * channels
    col, row = "c", "r"

    def lists(m):
        return tile_lists[m].reshape(-1), list_counts[m]

    def triangle(lr, m):
        lr = exchange(lr.reshape(devices, 2 * chans, cells)).reshape(tiles, 2 * chans, side, side)
        kernel = functools.partial(triangle_kernel, m == 1, tiles, kmax, chans)
        prod = tile_call(kernel, f"triangle{m}", lists(m), (lr,), (tiles, chans, side, side), [])
        return lr, exchange(prod.reshape(tiles, chans, cells)).reshape(channels, cells)

    def triangle_back(lr, gprod, m):
        gprod = exchange(gprod.reshape(devices, chans, cells)).reshape(tiles, chans, side, side)
        kernel = functools.partial(triangle_back_kernel, m == 1, tiles, kmax, chans)
        glr = tile_call(
            kernel, f"triangle_back{m}", lists(m), (lr, gprod), lr.shape, [pltpu.VMEM(lr.shape, F32)]
        )
        return exchange(glr.reshape(tiles, 2 * chans, cells)).reshape(wide, cells)

    def whole(*arrays):
        return [("w", array) for array in arrays]

    low_cells = (col, (channels, cells), BF16)
    lr_cells = (col, (wide, cells), BF16)
    square = ("w", (channels, channels), F32)
    broad = ("w", (channels, 2 * wide), F32)
    rows_out = (row, (cells, channels), BF16)

    (lr0,) = cellwise(first_kernel, "first", [(row, x)] + whole(*weights[0]), [lr_cells], cells)
    lr0, prod0 = triangle(lr0, 0)
    pair1, lr1 = cellwise(
        middle_kernel, "middle",
        [(row, x), (col, prod0)] + whole(w_gate[0], w_out[0], *weights[1]),
        [low_cells, lr_cells], cells,
    )
    lr1, prod1 = triangle(lr1, 1)
    new_pair, gprod1, glogit1, dgate1, dout1 = cellwise(
        top_kernel, "top",
        [(col, pair1), (col, prod1), (row, cot)] + whole(w_gate[1], w_out[1]),
        [rows_out, low_cells, low_cells, square, square], cells,
    )
    glr1 = triangle_back(lr1, gprod1, 1)
    upstream, gprod0, glogit0, dpair1, dgate0, dout0 = cellwise(
        turn_kernel, "turn",
        [(row if a is cot or a is x else col, a) for a in (pair1, cot, glr1, glogit1, x, prod0)]
        + whole(*weights[1], w_gate[1], w_gate[0], w_out[0]),
        [(col, (channels, cells), F32), low_cells, low_cells, broad, square, square], cells,
    )
    glr0 = triangle_back(lr0, gprod0, 0)
    d_pair, dpair0 = cellwise(
        last_kernel, "last",
        [(row, x), (col, upstream), (col, glr0), (col, glogit0)] + whole(*weights[0], w_gate[0]),
        [rows_out, broad], cells,
    )

    scale = 1.0 / math.sqrt(tiles * side * side)

    def scatter(*grads):
        joined = jnp.concatenate(grads, axis=1)
        return lax.psum_scatter(joined, "tile", scatter_dimension=0, tiled=True) * scale

    def unpermute(pair):
        pair = pair.reshape(-1, 2, devices, 2, chans).transpose(0, 3, 1, 2, 4)
        return pair.reshape(-1, 2 * wide)

    early = scatter(dpair1, dgate1, dout1, dgate0, dout0)
    late = scatter(dpair0)
    ends = [2 * wide + channels * n for n in range(5)]
    dgate1, dout1, dgate0, dout0 = [early[:, a:b] for a, b in zip(ends, ends[1:])]
    return (
        new_pair.reshape(pair_tiles.shape),
        d_pair.reshape(pair_tiles.shape),
        jnp.stack([unpermute(late), unpermute(early[:, : 2 * wide])]),
        jnp.stack([dgate0, dgate1]),
        jnp.stack([dout0, dout1]),
    )


def solution(mesh):
    cells = P(("groups", "tile"), None, None, None)
    in_specs = (cells, cells, P(), P(), P(), P(None, "groups", None, None), P(None, "groups"))
    grads = P("groups", "tile", None)
    return jax.shard_map(
        functools.partial(local, mesh.shape["tile"]), mesh=mesh, in_specs=in_specs,
        out_specs=(cells, cells, grads, grads, grads), check_vma=False,
    )
```

time: 946 us -> 574 us (0.61)
  other arithmetic: 170 us -> 3.3 us
  local copies, waits for them, and re-layouts: 229 us -> 80.3 us
  matrix products: 106 us -> 0 us
  blocking collectives: 63.1 us -> 148 us
  Pallas kernels: 0 us -> 75.6 us
  waiting for transfers between devices: 285 us -> 219 us
  starting transfers between devices: 67.7 us -> 31 us
    dot_general x30 -> x0, matrix products: 106 us -> none  [mixed_product(): jnp.einsum(pattern, one_side, other_side, preferred_element_type=jnp.floa...]
    all_to_all x2 -> x4, blocking collectives: 63.1 us -> 148 us  [exchange(): lax.all_to_all(array, 'tile', split_axis=0, concat_axis=0, tiled=True)]
    scatter-add x8 -> x0, other arithmetic: 75.7 us -> none  [the longest x4 38.1 us: accumulate(): totals[1].at[right_index].add(right_grad)]
    pallas_call x0 -> x9, Pallas kernels: none -> 75.6 us  [the longest x5 50.6 us: cellwise(): pl.pallas_call(kernel, name=name, grid=(cells // step,), in_specs=[spec(k...]
    convert_element_type x17 -> x0, other arithmetic: 60.2 us -> none  [the longest x4 9.92 us: triangle_back(): return (left_total.astype(jnp.bfloat16), right_total.astype(jnp.bfloat16))]
    convert_element_type x14 -> x0, local copies, waits for them, and re-layouts: 55.1 us -> none  [the longest x2 9.81 us: back_in(): right_flow = grad_right.astype(jnp.float32)]
    gather x16 -> x0, local copies, waits for them, and re-layouts: 53.7 us -> none  [the longest x4 15.1 us: accumulate(): left_live = jnp.take(left_chan, left_index, axis=0) * alive_mask]
    unnamed x138 -> x73, local copies, waits for them, and re-layouts: 88.3 us -> 34.7 us
  transfers between devices with their start and end apart: 13 -> 6, of which waited for: 11 -> 5; matrix products, arithmetic and copies ran while one was open for 11% -> 2% of each run, Pallas kernels for 0% -> 0%
where the time goes in v1:
time: 574 us; the launch traced here: 572 us
  waiting for transfers between devices  219 us (38%)
  blocking collectives  148 us (26%)
  local copies, waits for them, and re-layouts  80.3 us (14%)
  Pallas kernels  75.6 us (13%)
  starting transfers between devices  31 us (5%)
  between operations  14.4 us (3%)
    all_to_all x4, blocking collectives, exchange(): lax.all_to_all(array, 'tile', split_axis=0, concat_axis=0, tiled=True)  148 us
    reduce_scatter x2, waiting for transfers between devices, scatter(): lax.psum_scatter(joined, 'tile', scatter_dimension=0, tiled=True) * scale  115 us
    all_to_all x4, waiting for transfers between devices, exchange(): lax.all_to_all(array, 'tile', split_axis=0, concat_axis=0, tiled=True)  105 us
    pallas_call x5, Pallas kernels, cellwise(): pl.pallas_call(kernel, name=name, grid=(cells // step,), in_specs=[spec(k...  50.6 us
    unnamed x73, local copies, waits for them, and re-layouts  34.7 us
    all_to_all x4, starting transfers between devices, exchange(): lax.all_to_all(array, 'tile', split_axis=0, concat_axis=0, tiled=True)  30.9 us
    pallas_call x4, Pallas kernels, tile_call(): pl.pallas_call(kernel, name=name, in_specs=[pl.BlockSpec(memory_space=plt...  25 us
    reshape x2, local copies, waits for them, and re-layouts, triangle_back(): return exchange(glr.reshape(tiles, 2 * chans, cells)).reshape(wide, cells)  13.2 us
  transfers between devices with their start and end apart: 6, of which 5 were waited for; matrix products, arithmetic and copies ran while one was open for 2% of the time, Pallas kernels for 0%

profile of v1, /device:TPU:0, one launch (start us, length us, event | category | flops | bytes accessed | tf_op | source)
XLA Modules:
  0.0 572.2 jit_solution(18038755598850163087)
XLA Ops:
  7.2 1.1 copy.18
  8.4 1.2 copy-done.6
  9.6 5.4 first.1
  15.0 7.5 %all-to-all-start = ((bf16[16,16,4096]{2,1,0:T(8,128)(2,1)}), bf16[16,16,4096]{2,1,0:T(8,128)(2,1)S(1)}, u32[]{:S(2)}, u32[]{:S(2)}) async-start(bf16[16,16,4096]{2,1,0:T(8,128)(2,1)} %bitcast.7), calls=%async_computation | async-start | bytes 4194304 | tf_op jit(solution)/shard_map/all_to_all | solution.py:218
  22.8 40.9 %all-to-all-done = bf16[16,16,4096]{2,1,0:T(8,128)(2,1)S(1)} async-done(((bf16[16,16,4096]{2,1,0:T(8,128)(2,1)}), bf16[16,16,4096]{2,1,0:T(8,128)(2,1)S(1)}, u32[]{:S(2)}, u32[]{:S(2)}) %all-to-all-start) | async-done | bytes 2097184 | tf_op jit(solution)/shard_map/all_to_all | solution.py:218
  63.7 5.5 reshape.95.lr_ref
  69.2 2.2 copy-done
  71.4 4.9 triangle0.1
  76.2 2.5 reshape.96
  78.7 11.4 %all-to-all-start.1 = ((bf16[16,8,4096]{2,1,0:T(8,128)(2,1)}), bf16[16,8,4096]{2,1,0:T(8,128)(2,1)S(1)}, u32[]{:S(2)}, u32[]{:S(2)}) async-start(bf16[16,8,4096]{2,1,0:T(8,128)(2,1)} %reshape.96), calls=%async_computation.1 | async-start | bytes 2097152 | tf_op jit(solution)/shard_map/all_to_all | solution.py:218
  90.2 22.9 %all-to-all-done.1 = bf16[16,8,4096]{2,1,0:T(8,128)(2,1)S(1)} async-done(((bf16[16,8,4096]{2,1,0:T(8,128)(2,1)}), bf16[16,8,4096]{2,1,0:T(8,128)(2,1)S(1)}, u32[]{:S(2)}, u32[]{:S(2)}) %all-to-all-start.1) | async-done | bytes 1048608 | tf_op jit(solution)/shard_map/all_to_all | solution.py:218
  113.0 6.8 %middle.1 = (bf16[128,4096]{1,0:T(8,128)(2,1)S(1)}, bf16[256,4096]{1,0:T(8,128)(2,1)S(1)}) custom-call(bf16[4096,128]{1,0:T(8,128)(2,1)S(1)} %bitcast.54, bf16[128,4096]{1,0:T(8,128)(2,1)S(1)} %bitcast.57, bf16[128,128]{1,0:T(8,128)(2,1)S(1)} %get-tuple-element.51.wgate.wgate0, bf16[128,128]{1,0:T(8,128)(2,1)S(1)} %get-tuple-element.40.wout.wout0, ...), custom_call_target="tpu_custom_call" | custom-call | tf_op jit(solution)/shard_map/middle/pallas_call | solution.py:144
  120.8 1.4 copy-done.16
  122.2 6.9 %all-to-all-start.2 = ((bf16[16,16,4096]{2,1,0:T(8,128)(2,1)}), bf16[16,16,4096]{2,1,0:T(8,128)(2,1)}, u32[]{:S(2)}, u32[]{:S(2)}) async-start(bf16[16,16,4096]{2,1,0:T(8,128)(2,1)} %bitcast.64), calls=%async_computation.2 | async-start | bytes 4194304 | tf_op jit(solution)/shard_map/all_to_all | solution.py:218
  129.3 40.9 %all-to-all-done.2 = bf16[16,16,4096]{2,1,0:T(8,128)(2,1)} async-done(((bf16[16,16,4096]{2,1,0:T(8,128)(2,1)}), bf16[16,16,4096]{2,1,0:T(8,128)(2,1)}, u32[]{:S(2)}, u32[]{:S(2)}) %all-to-all-start.2) | async-done | bytes 2097184 | tf_op jit(solution)/shard_map/all_to_all | solution.py:218
  170.3 6.9 %reshape.99.lr_ref = bf16[16,16,64,64]{3,2,1,0:T(8,128)(2,1)} reshape(bf16[16,16,4096]{2,1,0:T(8,128)(2,1)} %all-to-all-done.2) | data formatting | bytes 4194304 | tf_op jit(solution)/shard_map/reshape | solution.py:237
  177.2 2.2 copy-done.2
  179.4 4.8 triangle1.1
  184.2 1.3 copy-done.8
  185.5 4.2 reshape.100
  189.7 36.2 %all_to_all.40 = bf16[16,8,4096]{2,1,0:T(8,128)(2,1)S(1)} all-to-all(bf16[16,8,4096]{2,1,0:T(8,128)(2,1)} %reshape.100), channel_id=1, replica_groups=mesh['groups'=2,'tile'=16] {'tile'}, dimensions={0} | all-to-all | bytes 2097152 | tf_op jit(solution)/shard_map/all_to_all | solution.py:218
  225.9 8.1 %top.1 = (bf16[4096,128]{1,0:T(8,128)(2,1)}, bf16[128,4096]{1,0:T(8,128)(2,1)S(1)}, bf16[128,4096]{1,0:T(8,128)(2,1)S(1)}, f32[128,128]{1,0:T(8,128)S(1)}, f32[128,128]{1,0:T(8,128)S(1)}) custom-call(bf16[128,4096]{1,0:T(8,128)(2,1)S(1)} %copy-done.12, bf16[128,4096]{1,0:T(8,128)(2,1)S(1)} %bitcast.61, bf16[4096,128]{1,0:T(8,128)(2,1)S(1)} %bitcast.62, ...), custom_call_target="tpu_custom_call" | custom-call | tf_op jit(solution)/shard_map/top/pallas_call | solution.py:144
  236.2 29.7 %all_to_all.41 = bf16[16,8,4096]{2,1,0:T(8,128)(2,1)} all-to-all(bf16[16,8,4096]{2,1,0:T(8,128)(2,1)S(1)} %bitcast.66), channel_id=1, replica_groups=mesh['groups'=2,'tile'=16] {'tile'}, dimensions={0} | all-to-all | bytes 2097152 | tf_op jit(solution)/shard_map/all_to_all | solution.py:218
  266.0 4.2 reshape.105.gprod_ref
  270.2 2.2 copy-done.3
  272.4 1.6 copy-done.9
  274.0 7.4 %triangle_back1.1 = bf16[16,16,64,64]{3,2,1,0:T(8,128)(2,1)S(1)} custom-call(s32[64]{0:T(128)S(1)} %reshape_squeeze.9.lists, s32[16]{0:T(128)S(1)} %get-tuple-element.49.counts, bf16[16,16,64,64]{3,2,1,0:T(8,128)(2,1)S(1)} %copy-done.3, bf16[16,8,64,64]{3,2,1,0:T(8,128)(2,1)S(1)} %copy-done.9), custom_call_target="tpu_custom_call" | custom-call | tf_op jit(solution)/shard_map/triangle_back1/pallas_call | solution.py:205
  281.4 2.0 copy-done.4
  283.4 6.6 %reshape.106 = bf16[16,16,4096]{2,1,0:T(8,128)(2,1)} reshape(bf16[16,16,64,64]{3,2,1,0:T(8,128)(2,1)} %copy-done.4) | data formatting | bytes 4194304 | tf_op jit(solution)/shard_map/reshape | solution.py:248
  290.0 52.4 %all_to_all.42 = bf16[16,16,4096]{2,1,0:T(8,128)(2,1)S(1)} all-to-all(bf16[16,16,4096]{2,1,0:T(8,128)(2,1)} %reshape.106), channel_id=1, replica_groups=mesh['groups'=2,'tile'=16] {'tile'}, dimensions={0} | all-to-all | bytes 4194304 | tf_op jit(solution)/shard_map/all_to_all | solution.py:218
  342.5 17.4 %turn.1 = (f32[128,4096]{1,0:T(8,128)S(1)}, bf16[128,4096]{1,0:T(8,128)(2,1)S(1)}, bf16[128,4096]{1,0:T(8,128)(2,1)S(1)}, f32[128,512]{1,0:T(8,128)S(1)}, f32[12...) custom-call(bf16[128,4096]{1,0:T(8,128)(2,1)S(1)} %copy-done.13, bf16[4096,128]{1,0:T(8,128)(2,1)S(1)} %bitcast.63, ...), custom_call_target="tpu_custom_call" | custom-call | tf_op jit(solution)/shard_map/turn/pallas_call | solution.py:144
  359.9 1.4 copy-done.14
  364.2 29.8 %all_to_all.43 = bf16[16,8,4096]{2,1,0:T(8,128)(2,1)} all-to-all(bf16[16,8,4096]{2,1,0:T(8,128)(2,1)S(1)} %bitcast.65), channel_id=1, replica_groups=mesh['groups'=2,'tile'=16] {'tile'}, dimensions={0} | all-to-all | bytes 2097152 | tf_op jit(solution)/shard_map/all_to_all | solution.py:218
  394.0 3.3 reshape.109.gprod_ref
  397.3 2.2 copy-done.1
  399.5 7.9 %triangle_back0.1 = bf16[16,16,64,64]{3,2,1,0:T(8,128)(2,1)S(1)} custom-call(s32[64]{0:T(128)S(1)} %reshape_squeeze.8.lists, s32[16]{0:T(128)S(1)} %get-tuple-element.50.counts, bf16[16,16,64,64]{3,2,1,0:T(8,128)(2,1)S(1)} %copy-done.1, bf16[16,8,64,64]{3,2,1,0:T(8,128)(2,1)S(1)} %reshape.109.gprod_ref), custom_call_target="tpu_custom_call" | custom-call | tf_op jit(solution)/shard_map/triangle_back0/pallas_call | solution.py:205
  407.4 2.0 copy-done.5
  409.3 6.6 %reshape.110 = bf16[16,16,4096]{2,1,0:T(8,128)(2,1)} reshape(bf16[16,16,64,64]{3,2,1,0:T(8,128)(2,1)} %copy-done.5) | data formatting | bytes 4194304 | tf_op jit(solution)/shard_map/reshape | solution.py:248
  416.0 5.1 all-to-all-start.7
  421.1 1.7 constant_dynamic-update-slice_fusion.4
  424.1 1.5 constant_dynamic-update-slice_fusion.1
  426.3 61.5 %reduce-scatter.5.cloned.1.call-done = f32[8,1024]{1,0:T(8,128)} async-done(((f32[128,1024]{1,0:T(8,128)}), f32[8,1024]{1,0:T(8,128)}) %reduce-scatter.5.cloned.1.call-update) | async-done | bytes 32784 | tf_op jit(solution)/shard_map/reduce_scatter | solution.py:290
  488.6 1.1 reshape.114
  489.8 1.7 copy.25
  492.6 1.6 copy-done.15
  494.1 1.2 copy-done.18
  495.4 12.9 %last.1 = (bf16[4096,128]{1,0:T(8,128)(2,1)}, f32[128,512]{1,0:T(8,128)S(1)}) custom-call(bf16[4096,128]{1,0:T(8,128)(2,1)S(1)} %bitcast.56, f32[128,4096]{1,0:T(8,128)S(1)} %copy-done.15, bf16[256,4096]{1,0:T(8,128)(2,1)S(1)} %bitcast.59, bf16[128,4096]{1,0:T(8,128)(2,1)S(1)} %copy-done.18, bf16[256,128]{1,0:T(8,128)(2,1)S(1)} %bitcast.70, ...), custom_call_target="tpu_custom_call" | custom-call | tf_op jit(solution)/shard_map/last/pallas_call | solution.py:144
  510.2 53.3 %reduce-scatter.3.cloned.1.call-done = f32[8,512]{1,0:T(8,128)} async-done(((f32[128,512]{1,0:T(8,128)}), f32[8,512]{1,0:T(8,128)}) %reduce-scatter.3.cloned.1.call-update) | async-done | bytes 16400 | tf_op jit(solution)/shard_map/reduce_scatter | solution.py:290
  (86 shorter events, 14.4 us)
Async XLA Ops:
  8.4 1.2 copy-start.6
  15.0 7.5 %copy-start.32 = (s32[2,16,2,2]{1,3,2,0:T(2,128)S(1)}, s32[2,16,2,2]{1,3,2,0:T(2,128)}, u32[]{:S(2)}) copy-start(s32[2,16,2,2]{1,3,2,0:T(2,128)} %param.12) | copy-start | bytes 1540
  15.0 7.8 %copy-start.33 = (s32[2,16]{1,0:T(2,128)S(1)}, s32[2,16]{1,0:T(2,128)}, u32[]{:S(2)}) copy-start(s32[2,16]{1,0:T(2,128)} %param.13) | copy-start | bytes 388
  15.0 48.6 %all-to-all-start = ((bf16[16,16,4096]{2,1,0:T(8,128)(2,1)}), bf16[16,16,4096]{2,1,0:T(8,128)(2,1)S(1)}, u32[]{:S(2)}, u32[]{:S(2)}) async-start(bf16[16,16,4096]{2,1,0:T(8,128)(2,1)} %bitcast.7), calls=%async_computation | async-start | bytes 4194304 | tf_op jit(solution)/shard_map/all_to_all | solution.py:218
  69.2 2.2 copy-start
  76.2 13.9 %copy-start.30 = (bf16[2,128,128]{2,1,0:T(8,128)(2,1)S(1)}, bf16[2,128,128]{2,1,0:T(8,128)(2,1)}, u32[]{:S(2)}) copy-start(bf16[2,128,128]{2,1,0:T(8,128)(2,1)} %param.11) | copy-start | bytes 196612
  76.2 13.9 %copy-start.31 = (bf16[2,128,128]{2,1,0:T(8,128)(2,1)S(1)}, bf16[2,128,128]{2,1,0:T(8,128)(2,1)}, u32[]{:S(2)}) copy-start(bf16[2,128,128]{2,1,0:T(8,128)(2,1)} %param.10) | copy-start | bytes 196612
  78.7 34.3 %copy-start.7 = (bf16[1,64,64,128]{3,2,1,0:T(8,128)(2,1)S(1)}, bf16[1,64,64,128]{3,2,1,0:T(8,128)(2,1)}, u32[]{:S(2)}) copy-start(bf16[1,64,64,128]{3,2,1,0:T(8,128)(2,1)} %param.7) | copy-start | bytes 3145732
  78.7 34.3 %all-to-all-start.1 = ((bf16[16,8,4096]{2,1,0:T(8,128)(2,1)}), bf16[16,8,4096]{2,1,0:T(8,128)(2,1)S(1)}, u32[]{:S(2)}, u32[]{:S(2)}) async-start(bf16[16,8,4096]{2,1,0:T(8,128)(2,1)} %reshape.96), calls=%async_computation.1 | async-start | bytes 2097152 | tf_op jit(solution)/shard_map/all_to_all | solution.py:218
  119.8 1.0 copy-start.11
  120.8 1.4 copy-start.16
  122.2 48.1 %all-to-all-start.2 = ((bf16[16,16,4096]{2,1,0:T(8,128)(2,1)}), bf16[16,16,4096]{2,1,0:T(8,128)(2,1)}, u32[]{:S(2)}, u32[]{:S(2)}) async-start(bf16[16,16,4096]{2,1,0:T(8,128)(2,1)} %bitcast.64), calls=%async_computation.2 | async-start | bytes 4194304 | tf_op jit(solution)/shard_map/all_to_all | solution.py:218
  177.2 2.2 copy-start.2
  184.2 1.3 copy-start.8
  185.5 40.4 %copy-start.10 = (bf16[1,64,64,128]{3,2,1,0:T(8,128)(2,1)S(1)}, bf16[1,64,64,128]{3,2,1,0:T(8,128)(2,1)}, u32[]{:S(2)}) copy-start(bf16[1,64,64,128]{3,2,1,0:T(8,128)(2,1)} %param.8) | copy-start | bytes 3145732
  189.7 36.2 %copy-start.12 = (bf16[128,4096]{1,0:T(8,128)(2,1)S(1)}, bf16[128,4096]{1,0:T(8,128)(2,1)}, u32[]{:S(2)}) copy-start(bf16[128,4096]{1,0:T(8,128)(2,1)} %copy-done.11) | copy-start | bytes 3145732
  234.0 1.0 copy-start.19
  235.0 0.6 copy-start.23
  235.6 0.6 copy-start.25
  270.2 2.2 copy-start.3
  272.4 1.6 copy-start.9
  281.4 2.0 copy-start.4
  290.0 52.4 %copy-start.13 = (bf16[128,4096]{1,0:T(8,128)(2,1)S(1)}, bf16[128,4096]{1,0:T(8,128)(2,1)}, u32[]{:S(2)}) copy-start(bf16[128,4096]{1,0:T(8,128)(2,1)} %copy-done.11) | copy-start | bytes 3145732
  290.0 52.4 %copy-start.20 = (bf16[128,4096]{1,0:T(8,128)(2,1)S(1)}, bf16[128,4096]{1,0:T(8,128)(2,1)}, u32[]{:S(2)}) copy-start(bf16[128,4096]{1,0:T(8,128)(2,1)} %copy-done.19) | copy-start | bytes 3145732
  359.9 1.4 copy-start.14
  361.2 1.0 copy-start.17
  362.2 0.7 copy-start.21
  362.9 0.6 copy-start.27
  363.5 0.6 copy-start.29
  397.3 2.2 copy-start.1
  407.4 2.0 copy-start.5
  415.9 6.9 %copy-start.26 = (f32[128,128]{1,0:T(8,128)S(1)}, f32[128,128]{1,0:T(8,128)}, u32[]{:S(2)}) copy-start(f32[128,128]{1,0:T(8,128)} %copy-done.25) | copy-start | bytes 196612
  416.0 7.5 %copy-start.24 = (f32[128,128]{1,0:T(8,128)S(1)}, f32[128,128]{1,0:T(8,128)}, u32[]{:S(2)}) copy-start(f32[128,128]{1,0:T(8,128)} %copy-done.23) | copy-start | bytes 196612
  416.0 9.6 %copy-start.28 = (f32[128,128]{1,0:T(8,128)S(1)}, f32[128,128]{1,0:T(8,128)}, u32[]{:S(2)}) copy-start(f32[128,128]{1,0:T(8,128)} %copy-done.27) | copy-start | bytes 196612
  416.0 76.6 %all-to-all-start.7 = ((bf16[16,16,4096]{2,1,0:T(8,128)(2,1)}), bf16[16,16,4096]{2,1,0:T(8,128)(2,1)S(1)}, u32[]{:S(2)}, u32[]{:S(2)}) async-start(bf16[16,16,4096]{2,1,0:T(8,128)(2,1)} %reshape.110), calls=%async_computation.7 | async-start | bytes 4194304 | tf_op jit(solution)/shard_map/all_to_all | solution.py:218
  421.1 66.8 %reduce-scatter.5.cloned.1.call-start = ((), (), s32[]{:S(2)}) async-start(), calls=%async_computation.11 | async-start | bytes 557056 | tf_op jit(solution)/shard_map/reduce_scatter | solution.py:290
  426.3 137.2 %reduce-scatter.3.cloned.1.call-start = ((), (), s32[]{:S(2)}) async-start(), calls=%async_computation.10 | async-start | bytes 278528 | tf_op jit(solution)/shard_map/reduce_scatter | solution.py:290
  492.5 1.6 copy-start.15
  494.1 1.2 copy-start.18
  508.3 0.7 copy-start.22
Sparse Core Ops, SparseCore 0:
  426.4 61.4 reduce-scatter.4
  509.1 54.2 reduce-scatter.2

commit v2 on v1

--- a/solution.py
+++ b/solution.py
@@ -214,8 +214,74 @@
     )(*scalars, *arrays)
 
 
-def exchange(array):
-    return lax.all_to_all(array, "tile", split_axis=0, concat_axis=0, tiled=True)
+def exchange_kernel(amount, devices, *refs):
+    sources, targets = refs[:amount], refs[amount : 2 * amount]
+    send_sem, recv_sem, own_sem = refs[2 * amount :]
+    me = lax.axis_index("tile")
+    barrier = pltpu.get_barrier_semaphore()
+
+    def greet(offset, _):
+        peer = lax.rem(me + offset, devices)
+        pl.semaphore_signal(
+            barrier, inc=1, device_id={"tile": peer}, device_id_type=pl.DeviceIdType.MESH
+        )
+        return 0
+
+    lax.fori_loop(1, devices, greet, 0)
+    own = [
+        pltpu.make_async_copy(source.at[me], target.at[me], own_sem.at[n])
+        for n, (source, target) in enumerate(zip(sources, targets))
+    ]
+    for copy in own:
+        copy.start()
+    pl.semaphore_wait(barrier, devices - 1)
+
+    def copies(offset):
+        peer = lax.rem(me + offset, devices)
+        return [
+            pltpu.make_async_remote_copy(
+                src_ref=source.at[peer],
+                dst_ref=target.at[me],
+                send_sem=send_sem.at[n, offset],
+                recv_sem=recv_sem.at[n, offset],
+                device_id={"tile": peer},
+                device_id_type=pl.DeviceIdType.MESH,
+            )
+            for n, (source, target) in enumerate(zip(sources, targets))
+        ]
+
+    def begin(place, _):
+        far = (place + 1) // 2
+        for copy in copies(devices // 2 + far * (1 - 2 * lax.rem(place, 2))):
+            copy.start()
+        return 0
+
+    def finish(offset, _):
+        for copy in copies(offset):
+            copy.wait()
+        return 0
+
+    lax.fori_loop(0, devices - 1, begin, 0)
+    lax.fori_loop(1, devices, finish, 0)
+    for copy in own:
+        copy.wait()
+
+
+def exchange(number, *arrays):
+    amount, devices = len(arrays), arrays[0].shape[0]
+    return pl.pallas_call(
+        functools.partial(exchange_kernel, amount, devices),
+        name=f"exchange{number}",
+        in_specs=[pl.BlockSpec(memory_space=pl.ANY)] * amount,
+        out_specs=[pl.BlockSpec(memory_space=pl.ANY)] * amount,
+        out_shape=[jax.ShapeDtypeStruct(a.shape, a.dtype) for a in arrays],
+        scratch_shapes=[
+            pltpu.SemaphoreType.DMA((amount, devices)),
+            pltpu.SemaphoreType.DMA((amount, devices)),
+            pltpu.SemaphoreType.DMA((amount,)),
+        ],
+        compiler_params=pltpu.CompilerParams(collective_id=number, has_side_effects=True),
+    )(*arrays)
 
 
 def local(devices, pair_tiles, cotangent, w_pair, w_gate, w_out, tile_lists, list_counts):
@@ -234,18 +300,25 @@
         return tile_lists[m].reshape(-1), list_counts[m]
 
     def triangle(lr, m):
-        lr = exchange(lr.reshape(devices, 2 * chans, cells)).reshape(tiles, 2 * chans, side, side)
+        (lr,) = exchange(2 * m, lr.reshape(devices, 2 * chans, cells))
+        lr = lr.reshape(tiles, 2 * chans, side, side)
         kernel = functools.partial(triangle_kernel, m == 1, tiles, kmax, chans)
         prod = tile_call(kernel, f"triangle{m}", lists(m), (lr,), (tiles, chans, side, side), [])
-        return lr, exchange(prod.reshape(tiles, chans, cells)).reshape(channels, cells)
-
-    def triangle_back(lr, gprod, m):
-        gprod = exchange(gprod.reshape(devices, chans, cells)).reshape(tiles, chans, side, side)
+        (prod,) = exchange(2 * m + 1, prod.reshape(tiles, chans, cells))
+        return lr, prod.reshape(channels, cells)
+
+    def triangle_back(lr, gprod, m, *others):
+        (gprod,) = exchange(4 + 2 * m, gprod.reshape(devices, chans, cells))
+        gprod = gprod.reshape(tiles, chans, side, side)
         kernel = functools.partial(triangle_back_kernel, m == 1, tiles, kmax, chans)
         glr = tile_call(
             kernel, f"triangle_back{m}", lists(m), (lr, gprod), lr.shape, [pltpu.VMEM(lr.shape, F32)]
         )
-        return exchange(glr.reshape(tiles, 2 * chans, cells)).reshape(wide, cells)
+        glr, *others = exchange(5 + 2 * m, glr.reshape(tiles, 2 * chans, cells), *others)
+        return glr.reshape(wide, cells), *others
+
+    def by_rows(grad):
+        return grad.reshape(devices, channels // devices, -1)
 
     def whole(*arrays):
         return [("w", array) for array in arrays]
@@ -269,14 +342,15 @@
         [(col, pair1), (col, prod1), (row, cot)] + whole(w_gate[1], w_out[1]),
         [rows_out, low_cells, low_cells, square, square], cells,
     )
-    glr1 = triangle_back(lr1, gprod1, 1)
+    (glr1,) = triangle_back(lr1, gprod1, 1)
     upstream, gprod0, glogit0, dpair1, dgate0, dout0 = cellwise(
         turn_kernel, "turn",
         [(row if a is cot or a is x else col, a) for a in (pair1, cot, glr1, glogit1, x, prod0)]
         + whole(*weights[1], w_gate[1], w_gate[0], w_out[0]),
         [(col, (channels, cells), F32), low_cells, low_cells, broad, square, square], cells,
     )
-    glr0 = triangle_back(lr0, gprod0, 0)
+    early = jnp.concatenate([dpair1, dgate1, dout1, dgate0, dout0], axis=1)
+    glr0, early = triangle_back(lr0, gprod0, 0, by_rows(early))
     d_pair, dpair0 = cellwise(
         last_kernel, "last",
         [(row, x), (col, upstream), (col, glr0), (col, glogit0)] + whole(*weights[0], w_gate[0]),
@@ -285,16 +359,12 @@
 
     scale = 1.0 / math.sqrt(tiles * side * side)
 
-    def scatter(*grads):
-        joined = jnp.concatenate(grads, axis=1)
-        return lax.psum_scatter(joined, "tile", scatter_dimension=0, tiled=True) * scale
-
     def unpermute(pair):
         pair = pair.reshape(-1, 2, devices, 2, chans).transpose(0, 3, 1, 2, 4)
         return pair.reshape(-1, 2 * wide)
 
-    early = scatter(dpair1, dgate1, dout1, dgate0, dout0)
-    late = scatter(dpair0)
+    early = jnp.sum(early, axis=0) * scale
+    late = jnp.sum(exchange(8, by_rows(dpair0))[0], axis=0) * scale
     ends = [2 * wide + channels * n for n in range(5)]
     dgate1, dout1, dgate0, dout0 = [early[:, a:b] for a, b in zip(ends, ends[1:])]
     return (

time: 574 us -> 493 us (0.86)
  Pallas kernels: 75.6 us -> 407 us
  waiting for transfers between devices: 219 us -> 0 us
  blocking collectives: 148 us -> 0 us
  starting transfers between devices: 31 us -> 0 us
  between operations: 14.4 us -> 1.17 us
    pallas_call x0 -> x9, Pallas kernels: none -> 332 us  [exchange(): pl.pallas_call(functools.partial(exchange_kernel, amount, devices), name=...]
    all_to_all x4 -> x0, blocking collectives: 148 us -> none  [exchange(): lax.all_to_all(array, 'tile', split_axis=0, concat_axis=0, tiled=True)]
    reduce_scatter x2 -> x0, waiting for transfers between devices: 115 us -> none  [scatter(): lax.psum_scatter(joined, 'tile', scatter_dimension=0, tiled=True) * scale]
    all_to_all x4 -> x0, waiting for transfers between devices: 105 us -> none  [exchange(): lax.all_to_all(array, 'tile', split_axis=0, concat_axis=0, tiled=True)]
    all_to_all x4 -> x0, starting transfers between devices: 30.9 us -> none  [exchange(): lax.all_to_all(array, 'tile', split_axis=0, concat_axis=0, tiled=True)]
    unnamed x73 -> x83, local copies, waits for them, and re-layouts: 34.7 us -> 36.9 us
  transfers between devices with their start and end apart: 6 -> 0, of which waited for: 5 -> 0; matrix products, arithmetic and copies ran while one was open for 2% -> 0% of each run, Pallas kernels for 0% -> 0%
where the time goes in v2:
time: 493 us; the launch traced here: 491 us
  Pallas kernels  407 us (83%)
  local copies, waits for them, and re-layouts  79.5 us (16%)
    pallas_call x9, Pallas kernels, exchange(): pl.pallas_call(functools.partial(exchange_kernel, amount, devices), name=...  332 us
    pallas_call x5, Pallas kernels, cellwise(): pl.pallas_call(kernel, name=name, grid=(cells // step,), in_specs=[spec(k...  49.4 us
    unnamed x83, local copies, waits for them, and re-layouts  36.9 us
    pallas_call x4, Pallas kernels, tile_call(): pl.pallas_call(kernel, name=name, in_specs=[pl.BlockSpec(memory_space=plt...  25.3 us
    reshape x2, local copies, waits for them, and re-layouts, triangle(): lr = lr.reshape(tiles, 2 * chans, side, side)  13.9 us
    reshape x2, local copies, waits for them, and re-layouts, triangle_back(): glr.reshape(tiles, 2 * chans, cells)  13.2 us

profile of v2, /device:TPU:0, one launch (start us, length us, event | category | flops | bytes accessed | tf_op | source)
XLA Modules:
  0.0 491.4 jit_solution(10418040150006282102)
XLA Ops:
  3.4 1.1 copy.17
  4.6 4.0 first.1
  8.7 1.4 copy-done.9
  10.0 47.5 %exchange0.1 = bf16[16,16,4096]{2,1,0:T(8,128)(2,1)} custom-call(bf16[16,16,4096]{2,1,0:T(8,128)(2,1)} %bitcast.61), custom_call_target="tpu_custom_call" | custom-call | tf_op jit(solution)/shard_map/exchange0/pallas_call | solution.py:272
  57.5 6.9 %reshape.102.lr_ref = bf16[16,16,64,64]{3,2,1,0:T(8,128)(2,1)} reshape(bf16[16,16,4096]{2,1,0:T(8,128)(2,1)} %exchange0.1) | data formatting | bytes 4194304 | tf_op jit(solution)/shard_map/reshape | solution.py:304
  64.4 2.2 copy-done
  66.6 4.9 triangle0.1
  71.5 2.5 reshape.103.refs_0_
  74.0 29.5 %exchange1.1 = bf16[16,8,4096]{2,1,0:T(8,128)(2,1)} custom-call(bf16[16,8,4096]{2,1,0:T(8,128)(2,1)} %reshape.103.refs_0_), custom_call_target="tpu_custom_call" | custom-call | tf_op jit(solution)/shard_map/exchange1/pallas_call | solution.py:272
  103.4 1.2 copy-done.7
  104.7 6.8 %middle.1 = (bf16[128,4096]{1,0:T(8,128)(2,1)S(1)}, bf16[256,4096]{1,0:T(8,128)(2,1)S(1)}) custom-call(bf16[4096,128]{1,0:T(8,128)(2,1)S(1)} %bitcast.56, bf16[128,4096]{1,0:T(8,128)(2,1)S(1)} %bitcast.59, bf16[128,128]{1,0:T(8,128)(2,1)S(1)} %get-tuple-element.55.wgate.wgate0, bf16[128,128]{1,0:T(8,128)(2,1)S(1)} %get-tuple-element.44.wout.wout0, ...), custom_call_target="tpu_custom_call" | custom-call | tf_op jit(solution)/shard_map/middle/pallas_call | solution.py:144
  112.4 1.4 copy-done.20
  113.8 46.8 %exchange2.1 = bf16[16,16,4096]{2,1,0:T(8,128)(2,1)} custom-call(bf16[16,16,4096]{2,1,0:T(8,128)(2,1)} %bitcast.67), custom_call_target="tpu_custom_call" | custom-call | tf_op jit(solution)/shard_map/exchange2/pallas_call | solution.py:272
  160.6 7.0 %reshape.106.lr_ref = bf16[16,16,64,64]{3,2,1,0:T(8,128)(2,1)} reshape(bf16[16,16,4096]{2,1,0:T(8,128)(2,1)} %exchange2.1) | data formatting | bytes 4194304 | tf_op jit(solution)/shard_map/reshape | solution.py:304
  167.6 2.2 copy-done.2
  169.8 4.8 triangle1.1
  174.6 2.5 reshape.107.refs_0_
  177.0 29.9 %exchange3.1 = bf16[16,8,4096]{2,1,0:T(8,128)(2,1)} custom-call(bf16[16,8,4096]{2,1,0:T(8,128)(2,1)} %reshape.107.refs_0_), custom_call_target="tpu_custom_call" | custom-call | tf_op jit(solution)/shard_map/exchange3/pallas_call | solution.py:272
  207.0 1.2 copy-done.11
  208.2 8.2 %top.1 = (bf16[4096,128]{1,0:T(8,128)(2,1)}, bf16[128,4096]{1,0:T(8,128)(2,1)S(1)}, bf16[128,4096]{1,0:T(8,128)(2,1)S(1)}, f32[128,128]{1,0:T(8,128)S(1)}, f32[128,128]{1,0:T(8,128)S(1)}) custom-call(bf16[128,4096]{1,0:T(8,128)(2,1)S(1)} %copy-done.15, bf16[128,4096]{1,0:T(8,128)(2,1)S(1)} %bitcast.63, bf16[4096,128]{1,0:T(8,128)(2,1)S(1)} %bitcast.64, ...), custom_call_target="tpu_custom_call" | custom-call | tf_op jit(solution)/shard_map/top/pallas_call | solution.py:144
  216.4 1.0 copy-done.24
  217.3 1.0 copy-done.25
  219.6 27.2 %exchange6.1 = bf16[16,8,4096]{2,1,0:T(8,128)(2,1)} custom-call(bf16[16,8,4096]{2,1,0:T(8,128)(2,1)} %bitcast.69), custom_call_target="tpu_custom_call" | custom-call | tf_op jit(solution)/shard_map/exchange6/pallas_call | solution.py:272
  246.8 3.3 reshape.112.gprod_ref
  250.1 2.2 copy-done.3
  252.2 7.7 %triangle_back1.1 = bf16[16,16,64,64]{3,2,1,0:T(8,128)(2,1)S(1)} custom-call(s32[64]{0:T(128)S(1)} %reshape_squeeze.9.lists, s32[16]{0:T(128)S(1)} %get-tuple-element.53.counts, bf16[16,16,64,64]{3,2,1,0:T(8,128)(2,1)S(1)} %copy-done.3, bf16[16,8,64,64]{3,2,1,0:T(8,128)(2,1)S(1)} %reshape.112.gprod_ref), custom_call_target="tpu_custom_call" | custom-call | tf_op jit(solution)/shard_map/triangle_back1/pallas_call | solution.py:205
  259.9 2.0 copy-done.4
  262.0 6.6 %reshape.113.refs_0_ = bf16[16,16,4096]{2,1,0:T(8,128)(2,1)} reshape(bf16[16,16,64,64]{3,2,1,0:T(8,128)(2,1)} %copy-done.4) | data formatting | bytes 4194304 | tf_op jit(solution)/shard_map/reshape | solution.py:317
  268.6 46.8 %exchange7.1 = bf16[16,16,4096]{2,1,0:T(8,128)(2,1)} custom-call(bf16[16,16,4096]{2,1,0:T(8,128)(2,1)} %reshape.113.refs_0_), custom_call_target="tpu_custom_call" | custom-call | tf_op jit(solution)/shard_map/exchange7/pallas_call | solution.py:272
  315.4 1.6 copy-done.10
  317.0 1.2 copy-done.16
  318.2 1.2 copy-done.26
  319.4 17.5 %turn.1 = (f32[128,4096]{1,0:T(8,128)S(1)}, bf16[128,4096]{1,0:T(8,128)(2,1)S(1)}, bf16[128,4096]{1,0:T(8,128)(2,1)S(1)}, f32[128,512]{1,0:T(8,128)S(1)}, f32[12...) custom-call(bf16[128,4096]{1,0:T(8,128)(2,1)S(1)} %copy-done.16, bf16[4096,128]{1,0:T(8,128)(2,1)S(1)} %bitcast.65, ...), custom_call_target="tpu_custom_call" | custom-call | tf_op jit(solution)/shard_map/turn/pallas_call | solution.py:144
  336.9 1.4 copy-done.17
  339.3 1.0 copy-done.23
  342.2 30.1 %exchange4.1 = bf16[16,8,4096]{2,1,0:T(8,128)(2,1)} custom-call(bf16[16,8,4096]{2,1,0:T(8,128)(2,1)} %bitcast.68), custom_call_target="tpu_custom_call" | custom-call | tf_op jit(solution)/shard_map/exchange4/pallas_call | solution.py:272
  373.3 3.3 reshape.116.gprod_ref
  376.5 2.2 copy-done.1
  378.7 7.9 %triangle_back0.1 = bf16[16,16,64,64]{3,2,1,0:T(8,128)(2,1)S(1)} custom-call(s32[64]{0:T(128)S(1)} %reshape_squeeze.8.lists, s32[16]{0:T(128)S(1)} %get-tuple-element.54.counts, bf16[16,16,64,64]{3,2,1,0:T(8,128)(2,1)S(1)} %copy-done.1, bf16[16,8,64,64]{3,2,1,0:T(8,128)(2,1)S(1)} %reshape.116.gprod_ref), custom_call_target="tpu_custom_call" | custom-call | tf_op jit(solution)/shard_map/triangle_back0/pallas_call | solution.py:205
  386.7 2.0 copy-done.5
  388.7 6.6 %reshape.117.refs_0_ = bf16[16,16,4096]{2,1,0:T(8,128)(2,1)} reshape(bf16[16,16,64,64]{3,2,1,0:T(8,128)(2,1)} %copy-done.5) | data formatting | bytes 4194304 | tf_op jit(solution)/shard_map/reshape | solution.py:317
  395.3 57.2 %exchange5.1 = (bf16[16,16,4096]{2,1,0:T(8,128)(2,1)}, f32[16,8,1024]{2,1,0:T(8,128)}) custom-call(bf16[16,16,4096]{2,1,0:T(8,128)(2,1)} %reshape.117.refs_0_, f32[16,8,1024]{2,1,0:T(8,128)} %bitcast.79), custom_call_target="tpu_custom_call" | custom-call | tf_op jit(solution)/shard_map/exchange5/pallas_call | solution.py:272
  452.5 1.6 copy-done.19
  454.0 1.2 copy-done.22
  455.3 12.9 %last.1 = (bf16[4096,128]{1,0:T(8,128)(2,1)}, f32[128,512]{1,0:T(8,128)S(1)}) custom-call(bf16[4096,128]{1,0:T(8,128)(2,1)S(1)} %bitcast.58, f32[128,4096]{1,0:T(8,128)S(1)} %copy-done.18, bf16[256,4096]{1,0:T(8,128)(2,1)S(1)} %bitcast.66, bf16[128,4096]{1,0:T(8,128)(2,1)S(1)} %copy-done.22, bf16[256,128]{1,0:T(8,128)(2,1)S(1)} %bitcast.73, ...), custom_call_target="tpu_custom_call" | custom-call | tf_op jit(solution)/shard_map/last/pallas_call | solution.py:144
  468.9 17.4 %exchange8.1 = f32[16,8,512]{2,1,0:T(8,128)} custom-call(f32[16,8,512]{2,1,0:T(8,128)} %bitcast.78), custom_call_target="tpu_custom_call" | custom-call | tf_op jit(solution)/shard_map/exchange8/pallas_call | solution.py:272
  486.3 1.0 reduce_sum.18
  487.2 1.1 reduce_sum.19
  (89 shorter events, 12.6 us)
Async XLA Ops:
  0.6 4.0 copy-start.6
  8.7 1.4 copy-start.9
  64.4 2.2 copy-start
  103.4 1.2 copy-start.7
  111.5 1.0 copy-start.14
  112.4 1.4 copy-start.20
  167.6 2.2 copy-start.2
  177.0 29.9 %copy-start.12 = (bf16[1,64,64,128]{3,2,1,0:T(8,128)(2,1)S(1)}, bf16[1,64,64,128]{3,2,1,0:T(8,128)(2,1)}, u32[]{:S(2)}) copy-start(bf16[1,64,64,128]{3,2,1,0:T(8,128)(2,1)} %param.8) | copy-start | bytes 3145732
  177.0 29.9 %copy-start.15 = (bf16[128,4096]{1,0:T(8,128)(2,1)S(1)}, bf16[128,4096]{1,0:T(8,128)(2,1)}, u32[]{:S(2)}) copy-start(bf16[128,4096]{1,0:T(8,128)(2,1)} %copy-done.14) | copy-start | bytes 3145732
  207.0 1.2 copy-start.11
  216.3 1.0 copy-start.24
  217.3 1.0 copy-start.25
  218.3 0.6 copy-start.30
  218.9 0.6 copy-start.32
  250.0 2.2 copy-start.3
  259.9 2.0 copy-start.4
  268.6 46.8 %copy-start.8 = (bf16[16,8,4096]{2,1,0:T(8,128)(2,1)S(1)}, bf16[16,8,4096]{2,1,0:T(8,128)(2,1)}, u32[]{:S(2)}) copy-start(bf16[16,8,4096]{2,1,0:T(8,128)(2,1)} %exchange1.1) | copy-start | bytes 3145732
  268.6 46.8 %copy-start.13 = (bf16[1,64,64,128]{3,2,1,0:T(8,128)(2,1)S(1)}, bf16[1,64,64,128]{3,2,1,0:T(8,128)(2,1)}, u32[]{:S(2)}) copy-start(bf16[1,64,64,128]{3,2,1,0:T(8,128)(2,1)} %param.8) | copy-start | bytes 3145732
  315.4 1.6 copy-start.10
  317.0 1.2 copy-start.16
  318.2 1.2 copy-start.26
  336.9 1.4 copy-start.17
  338.3 1.0 copy-start.21
  339.3 1.0 copy-start.23
  340.2 0.7 copy-start.27
  340.9 0.6 copy-start.34
  341.6 0.6 copy-start.36
  342.2 30.2 %copy-start.33 = (f32[128,128]{1,0:T(8,128)S(1)}, f32[128,128]{1,0:T(8,128)}, u32[]{:S(2)}) copy-start(f32[128,128]{1,0:T(8,128)} %copy-done.32) | copy-start | bytes 196612
  342.2 30.2 %copy-start.31 = (f32[128,128]{1,0:T(8,128)S(1)}, f32[128,128]{1,0:T(8,128)}, u32[]{:S(2)}) copy-start(f32[128,128]{1,0:T(8,128)} %copy-done.30) | copy-start | bytes 196612
  342.2 30.1 %copy-start.28 = (f32[128,512]{1,0:T(8,128)S(1)}, f32[128,512]{1,0:T(8,128)}, u32[]{:S(2)}) copy-start(f32[128,512]{1,0:T(8,128)} %copy-done.27) | copy-start | bytes 786436
  342.2 30.2 %copy-start.37 = (f32[128,128]{1,0:T(8,128)S(1)}, f32[128,128]{1,0:T(8,128)}, u32[]{:S(2)}) copy-start(f32[128,128]{1,0:T(8,128)} %copy-done.36) | copy-start | bytes 196612
  342.2 30.2 %copy-start.35 = (f32[128,128]{1,0:T(8,128)S(1)}, f32[128,128]{1,0:T(8,128)}, u32[]{:S(2)}) copy-start(f32[128,128]{1,0:T(8,128)} %copy-done.34) | copy-start | bytes 196612
  372.5 0.8 copy-start.38
  376.5 2.2 copy-start.1
  386.7 2.0 copy-start.5
  395.3 57.2 %copy-start.18 = (f32[128,4096]{1,0:T(8,128)S(1)}, f32[128,4096]{1,0:T(8,128)}, u32[]{:S(2)}) copy-start(f32[128,4096]{1,0:T(8,128)} %copy-done.17) | copy-start | bytes 6291460
  452.5 1.6 copy-start.19
  454.0 1.2 copy-start.22
  468.2 0.7 copy-start.29

commit v3 on v2

--- a/solution.py
+++ b/solution.py
@@ -92,7 +92,13 @@
 
 
 def turned(ref):
-    return ref[...].astype(F32).T
+    values = jnp.swapaxes(ref[...], 0, 1).astype(F32)
+    return values.reshape(-1, values.shape[-1]).T
+
+
+def turn_back(ref, values):
+    _, rows, side, channels = ref.shape
+    ref[...] = jnp.swapaxes(values.T.reshape(rows, 2, side, channels), 0, 1).astype(ref.dtype)
 
 
 def first_kernel(x_ref, wv, ws, lr_ref):
@@ -110,7 +116,7 @@
 def top_kernel(pair_ref, prod_ref, cot_ref, wgate, wout, new_ref, gprod_ref, glogit_ref, dgate_ref, dout_ref):
     pair = pair_ref[...].astype(F32)
     parts = out_parts(pair, prod_ref, wgate, wout)
-    new_ref[...] = (pair + parts[1] * parts[5]).T.astype(BF16)
+    turn_back(new_ref, pair + parts[1] * parts[5])
     back_out(turned(cot_ref), parts, wout, gprod_ref, glogit_ref, dgate_ref, dout_ref)
 
 
@@ -128,7 +134,7 @@
 
 def last_kernel(x_ref, up_ref, glr_ref, glogit_ref, wv, ws, wgate, dx_ref, dpair_ref):
     grad = back_in(up_ref[...], turned(x_ref), glr_ref, glogit_ref, wv, ws, wgate, dpair_ref)
-    dx_ref[...] = grad.T.astype(BF16)
+    turn_back(dx_ref, grad)
 
 
 def cellwise(kernel, name, args, outs, cells):
@@ -136,7 +142,8 @@
 
     def spec(kind, shape):
         if kind == "r":
-            return pl.BlockSpec((step, shape[1]), lambda n: (n, 0))
+            _, _, side, channels = shape
+            return pl.BlockSpec((2, step // (2 * side), side, channels), lambda n: (0, n, 0, 0))
         if kind == "c":
             return pl.BlockSpec((shape[0], step), lambda n: (0, n))
         return pl.BlockSpec(shape, lambda n: (0, 0))
@@ -152,62 +159,80 @@
     )(*[array for _, array in args])
 
 
-def triangle_kernel(incoming, tiles, kmax, chans, lists, counts, lr_ref, prod_ref):
+def unfold(folded):
+    side = folded.shape[1] // 2
+    return jnp.concatenate([folded[:, :side], folded[:, side:]], axis=0)
+
+
+def fold(square):
+    half = square.shape[0] // 2
+    return jnp.concatenate([square[:half], square[half:]], axis=1)
+
+
+def triangle_kernel(incoming, tiles, kmax, lists, counts, lr_ref, prod_ref):
     dim = 0 if incoming else 1
 
     def one(tile, _):
-        def term(slot, chan):
+        def term(slot):
             base = (tile * kmax + slot) * 2
-            return dot(lr_ref[lists[base], chan], lr_ref[lists[base + 1], chans + chan], dim, dim)
-
-        used = counts[tile]
-        for chan in range(chans):
-            total = term(0, chan)
-            for slot in range(1, kmax):
-                total = total + jnp.where(slot < used, term(slot, chan), 0.0)
-            prod_ref[tile, chan] = total.astype(BF16)
-        return 0
-
-    lax.fori_loop(0, tiles, one, 0)
-
-
-def triangle_back_kernel(incoming, tiles, kmax, chans, lists, counts, lr_ref, gprod_ref, glr_ref, total):
+            left = unfold(lr_ref[lists[base], 0, 0])
+            return dot(left, unfold(lr_ref[lists[base + 1], 1, 0]), dim, dim)
+
+        total = term(0)
+        for slot in range(1, kmax):
+            total = total + jnp.where(slot < counts[tile], term(slot), 0.0)
+        prod_ref[tile, 0] = fold(total).astype(BF16)
+        return 0
+
+    lax.fori_loop(0, tiles, one, 0, unroll=8)
+
+
+def triangle_back_kernel(incoming, tiles, kmax, lists, counts, lr_ref, gprod_ref, glr_ref, total):
     total[...] = jnp.zeros_like(total)
 
     def one(tile, _):
+        grad = unfold(gprod_ref[tile, 0])
         for slot in range(kmax):
 
-            @pl.when(slot < counts[tile])
-            def _():
+            def add():
                 base = (tile * kmax + slot) * 2
                 x, y = lists[base], lists[base + 1]
-                for chan in range(chans):
-                    grad = gprod_ref[tile, chan]
-                    left, right = lr_ref[x, chan], lr_ref[y, chans + chan]
-                    if incoming:
-                        total[x, chan] += dot(right, grad, 1, 1)
-                        total[y, chans + chan] += dot(left, grad, 1, 0)
-                    else:
-                        total[x, chan] += dot(grad, right, 1, 0)
-                        total[y, chans + chan] += dot(grad, left, 0, 0)
-        return 0
-
-    lax.fori_loop(0, tiles, one, 0)
+                left, right = unfold(lr_ref[x, 0, 0]), unfold(lr_ref[y, 1, 0])
+                if incoming:
+                    total[0, x] += dot(right, grad, 1, 1)
+                    total[1, y] += dot(left, grad, 1, 0)
+                else:
+                    total[0, x] += dot(grad, right, 1, 0)
+                    total[1, y] += dot(grad, left, 0, 0)
+
+            if slot == 0:
+                add()
+            else:
+                pl.when(slot < counts[tile])(add)
+        return 0
+
+    lax.fori_loop(0, tiles, one, 0, unroll=4)
 
     def store(tile, _):
-        glr_ref[tile] = total[tile].astype(BF16)
-        return 0
-
-    lax.fori_loop(0, tiles, store, 0)
+        for which in range(2):
+            glr_ref[tile, which, 0] = fold(total[which, tile]).astype(BF16)
+        return 0
+
+    lax.fori_loop(0, tiles, store, 0, unroll=4)
 
 
 def tile_call(kernel, name, scalars, arrays, out_shape, scratch):
+    def spec(shape):
+        lead = len(shape) - 3
+        return pl.BlockSpec(shape[:lead] + (1,) + shape[-2:], lambda n: (0,) * lead + (n, 0, 0))
+
     return pl.pallas_call(
         kernel,
         name=name,
+        grid=(out_shape[-3],),
         in_specs=[pl.BlockSpec(memory_space=pltpu.SMEM)] * len(scalars)
-        + [pl.BlockSpec(memory_space=pltpu.VMEM)] * len(arrays),
-        out_specs=pl.BlockSpec(memory_space=pltpu.VMEM),
+        + [spec(array.shape) for array in arrays],
+        out_specs=spec(out_shape),
         out_shape=jax.ShapeDtypeStruct(out_shape, BF16),
         scratch_shapes=scratch,
         compiler_params=pltpu.CompilerParams(vmem_limit_bytes=VMEM_BYTES),
@@ -289,8 +314,8 @@
     cells = owned * side * side
     tiles, kmax = tile_lists.shape[1], tile_lists.shape[2]
     chans = channels // devices
-    x = pair_tiles.reshape(cells, channels)
-    cot = cotangent.reshape(cells, channels)
+    x = pair_tiles.reshape(2, side // 2, side, channels)
+    cot = cotangent.reshape(x.shape)
     weights = w_pair.reshape(2, channels, 2, 2, devices, chans)
     weights = weights.transpose(0, 3, 4, 2, 5, 1).reshape(2, 2, 2 * channels, channels)
     wide = 2 * channels
@@ -299,26 +324,27 @@
     def lists(m):
         return tile_lists[m].reshape(-1), list_counts[m]
 
+    folded = (side // 2, 2 * side)
+
     def triangle(lr, m):
         (lr,) = exchange(2 * m, lr.reshape(devices, 2 * chans, cells))
-        lr = lr.reshape(tiles, 2 * chans, side, side)
-        kernel = functools.partial(triangle_kernel, m == 1, tiles, kmax, chans)
-        prod = tile_call(kernel, f"triangle{m}", lists(m), (lr,), (tiles, chans, side, side), [])
+        lr = lr.reshape(tiles, 2, chans, *folded)
+        kernel = functools.partial(triangle_kernel, m == 1, tiles, kmax)
+        prod = tile_call(kernel, f"triangle{m}", lists(m), (lr,), (tiles, chans, *folded), [])
         (prod,) = exchange(2 * m + 1, prod.reshape(tiles, chans, cells))
         return lr, prod.reshape(channels, cells)
 
     def triangle_back(lr, gprod, m, *others):
         (gprod,) = exchange(4 + 2 * m, gprod.reshape(devices, chans, cells))
-        gprod = gprod.reshape(tiles, chans, side, side)
-        kernel = functools.partial(triangle_back_kernel, m == 1, tiles, kmax, chans)
-        glr = tile_call(
-            kernel, f"triangle_back{m}", lists(m), (lr, gprod), lr.shape, [pltpu.VMEM(lr.shape, F32)]
-        )
+        gprod = gprod.reshape(tiles, chans, *folded)
+        kernel = functools.partial(triangle_back_kernel, m == 1, tiles, kmax)
+        sums = pltpu.VMEM((2, tiles, side, side), F32)
+        glr = tile_call(kernel, f"triangle_back{m}", lists(m), (lr, gprod), lr.shape, [sums])
         glr, *others = exchange(5 + 2 * m, glr.reshape(tiles, 2 * chans, cells), *others)
         return glr.reshape(wide, cells), *others
 
     def by_rows(grad):
-        return grad.reshape(devices, channels // devices, -1)
+        return grad.astype(BF16).reshape(devices, channels // devices, -1)
 
     def whole(*arrays):
         return [("w", array) for array in arrays]
@@ -327,7 +353,7 @@
     lr_cells = (col, (wide, cells), BF16)
     square = ("w", (channels, channels), F32)
     broad = ("w", (channels, 2 * wide), F32)
-    rows_out = (row, (cells, channels), BF16)
+    rows_out = (row, x.shape, BF16)
 
     (lr0,) = cellwise(first_kernel, "first", [(row, x)] + whole(*weights[0]), [lr_cells], cells)
     lr0, prod0 = triangle(lr0, 0)
@@ -363,8 +389,8 @@
         pair = pair.reshape(-1, 2, devices, 2, chans).transpose(0, 3, 1, 2, 4)
         return pair.reshape(-1, 2 * wide)
 
-    early = jnp.sum(early, axis=0) * scale
-    late = jnp.sum(exchange(8, by_rows(dpair0))[0], axis=0) * scale
+    early = jnp.sum(early.astype(F32), axis=0) * scale
+    late = jnp.sum(exchange(8, by_rows(dpair0))[0].astype(F32), axis=0) * scale
     ends = [2 * wide + channels * n for n in range(5)]
     dgate1, dout1, dgate0, dout0 = [early[:, a:b] for a, b in zip(ends, ends[1:])]
     return (

time: 493 us -> 540 us (1.095)
  Pallas kernels: 407 us -> 472 us
  local copies, waits for them, and re-layouts: 79.5 us -> 58 us
    pallas_call x4, Pallas kernels: 25.3 us -> 97.6 us  [tile_call(): pl.pallas_call(kernel, name=name, grid=(out_shape[-3],), in_specs=[pl.Blo...]
    reshape x4 -> x0, local copies, waits for them, and re-layouts: 20.4 us -> none  [the longest x2 13.9 us: triangle(): lr = lr.reshape(tiles, 2 * chans, side, side)]
    pallas_call x9, Pallas kernels: 332 us -> 324 us  [exchange(): pl.pallas_call(functools.partial(exchange_kernel, amount, devices), name=...]
    unnamed x83 -> x77, local copies, waits for them, and re-layouts: 36.9 us -> 41 us
where the time goes in v3:
time: 540 us; the launch traced here: 539 us
  Pallas kernels  472 us (87%)
  local copies, waits for them, and re-layouts  58 us (11%)
  other arithmetic  8.56 us (2%)
    pallas_call x9, Pallas kernels, exchange(): pl.pallas_call(functools.partial(exchange_kernel, amount, devices), name=...  324 us
    pallas_call x4, Pallas kernels, tile_call(): pl.pallas_call(kernel, name=name, grid=(out_shape[-3],), in_specs=[pl.Blo...  97.6 us
    pallas_call x5, Pallas kernels, cellwise(): pl.pallas_call(kernel, name=name, grid=(cells // step,), in_specs=[spec(k...  50.2 us
    unnamed x77, local copies, waits for them, and re-layouts  41 us

profile of v3, /device:TPU:0, one launch (start us, length us, event | category | flops | bytes accessed | tf_op | source)
XLA Modules:
  0.0 539.4 jit_solution(15430339021269555763)
XLA Ops:
  3.4 1.1 copy.17
  4.6 4.1 first.1
  8.8 1.3 copy-done.7
  10.1 47.5 %exchange0.1 = bf16[16,16,4096]{2,1,0:T(8,128)(2,1)} custom-call(bf16[16,16,4096]{2,1,0:T(8,128)(2,1)} %bitcast.95), custom_call_target="tpu_custom_call" | custom-call | tf_op jit(solution)/shard_map/exchange0/pallas_call | solution.py:297
  57.6 2.1 copy.25
  59.7 7.4 %triangle0.1 = bf16[16,8,32,128]{3,2,1,0:T(8,128)(2,1)S(1)} custom-call(s32[64]{0:T(128)S(1)} %reshape_squeeze.8.lists, s32[16]{0:T(128)S(1)} %get-tuple-element.54.counts, bf16[16,2,8,32,128]{4,3,2,1,0:T(8,128)(2,1)S(1)} %bitcast.85), custom_call_target="tpu_custom_call" | custom-call | tf_op jit(solution)/shard_map/triangle0/pallas_call | solution.py:229
  68.1 2.3 reshape.111.refs_0_
  70.4 29.5 %exchange1.1 = bf16[16,8,4096]{2,1,0:T(8,128)(2,1)} custom-call(bf16[16,8,4096]{2,1,0:T(8,128)(2,1)} %reshape.111.refs_0_), custom_call_target="tpu_custom_call" | custom-call | tf_op jit(solution)/shard_map/exchange1/pallas_call | solution.py:297
  99.9 1.2 copy-done.3
  101.1 6.9 %middle.1 = (bf16[128,4096]{1,0:T(8,128)(2,1)S(1)}, bf16[256,4096]{1,0:T(8,128)(2,1)S(1)}) custom-call(bf16[2,32,64,128]{3,2,1,0:T(8,128)(2,1)S(1)} %bitcast.90, bf16[128,4096]{1,0:T(8,128)(2,1)S(1)} %bitcast.93, bf16[128,128]{1,0:T(8,128)(2,1)S(1)} %get-tuple-element.55.wgate.wgate0, bf16[128,128]{1,0:T(8,128)(2,1)S(1)} %get-tuple-element.44.wout.wout0, ...), custom_call_target="tpu_custom_call" | custom-call | tf_op jit(solution)/shard_map/middle/pallas_call | solution.py:151
  108.9 1.4 copy-done.20
  110.3 46.8 %exchange2.1 = bf16[16,16,4096]{2,1,0:T(8,128)(2,1)} custom-call(bf16[16,16,4096]{2,1,0:T(8,128)(2,1)} %bitcast.101), custom_call_target="tpu_custom_call" | custom-call | tf_op jit(solution)/shard_map/exchange2/pallas_call | solution.py:297
  157.1 2.1 copy.26
  159.2 8.4 %triangle1.1 = bf16[16,8,32,128]{3,2,1,0:T(8,128)(2,1)S(1)} custom-call(s32[64]{0:T(128)S(1)} %reshape_squeeze.9.lists, s32[16]{0:T(128)S(1)} %get-tuple-element.53.counts, bf16[16,2,8,32,128]{4,3,2,1,0:T(8,128)(2,1)S(1)} %bitcast.87), custom_call_target="tpu_custom_call" | custom-call | tf_op jit(solution)/shard_map/triangle1/pallas_call | solution.py:229
  167.6 1.3 copy-done
  170.0 2.3 reshape.115.refs_0_
  172.3 29.9 %exchange3.1 = bf16[16,8,4096]{2,1,0:T(8,128)(2,1)} custom-call(bf16[16,8,4096]{2,1,0:T(8,128)(2,1)} %reshape.115.refs_0_), custom_call_target="tpu_custom_call" | custom-call | tf_op jit(solution)/shard_map/exchange3/pallas_call | solution.py:297
  202.2 1.2 copy-done.9
  203.4 1.2 copy-done.12
  204.6 1.2 copy-done.15
  205.8 8.4 %top.1 = (bf16[2,32,64,128]{3,2,1,0:T(8,128)(2,1)}, bf16[128,4096]{1,0:T(8,128)(2,1)S(1)}, bf16[128,4096]{1,0:T(8,128)(2,1)S(1)}, f32[128,128]{1,0:T(8,128)S(1)}, f32[128,128]{1,0:T(8,128)S(1)}) custom-call(bf16[128,4096]{1,0:T(8,128)(2,1)S(1)} %copy-done.15, bf16[128,4096]{1,0:T(8,128)(2,1)S(1)} %bitcast.97, bf16[2,32,64,128]{3,2,1,0:T(8,128)(2,1)S(1)} %bitcast.98, ...), custom_call_target="tpu_custom_call" | custom-call | tf_op jit(solution)/shard_map/top/pallas_call | solution.py:151
  215.2 1.0 copy-done.25
  217.5 27.1 %exchange6.1 = bf16[16,8,4096]{2,1,0:T(8,128)(2,1)} custom-call(bf16[16,8,4096]{2,1,0:T(8,128)(2,1)} %bitcast.103), custom_call_target="tpu_custom_call" | custom-call | tf_op jit(solution)/shard_map/exchange6/pallas_call | solution.py:297
  244.7 1.6 copy.32
  246.6 38.4 %triangle_back1.1 = bf16[16,2,8,32,128]{4,3,2,1,0:T(8,128)(2,1)S(1)} custom-call(s32[64]{0:T(128)S(1)} %reshape_squeeze.9.lists, s32[16]{0:T(128)S(1)} %get-tuple-element.53.counts, bf16[16,2,8,32,128]{4,3,2,1,0:T(8,128)(2,1)S(1)} %bitcast.88, bf16[16,8,32,128]{3,2,1,0:T(8,128)(2,1)S(1)} %copy.32), custom_call_target="tpu_custom_call" | custom-call | tf_op jit(solution)/shard_map/triangle_back1/pallas_call | solution.py:229
  285.0 1.3 copy-done.5
  286.3 4.2 reshape.121.refs_0_
  290.5 46.8 %exchange7.1 = bf16[16,16,4096]{2,1,0:T(8,128)(2,1)} custom-call(bf16[16,16,4096]{2,1,0:T(8,128)(2,1)} %reshape.121.refs_0_), custom_call_target="tpu_custom_call" | custom-call | tf_op jit(solution)/shard_map/exchange7/pallas_call | solution.py:297
  337.3 1.2 copy-done.4
  338.5 1.6 copy-done.8
  340.1 1.2 copy-done.13
  341.3 1.2 copy-done.16
  342.5 1.2 copy-done.26
  343.8 17.6 %turn.1 = (f32[128,4096]{1,0:T(8,128)S(1)}, bf16[128,4096]{1,0:T(8,128)(2,1)S(1)}, bf16[128,4096]{1,0:T(8,128)(2,1)S(1)}, f32[128,512]{1,0:T(8,128)S(1)}, f32[12...) custom-call(bf16[128,4096]{1,0:T(8,128)(2,1)S(1)} %copy-done.16, bf16[2,32,64,128]{3,2,1,0:T(8,128)(2,1)S(1)} %bitcast.99, ...), custom_call_target="tpu_custom_call" | custom-call | tf_op jit(solution)/shard_map/turn/pallas_call | solution.py:151
  361.4 1.3 copy-done.17
  362.7 1.0 copy-done.21
  366.6 29.9 %exchange4.1 = bf16[16,8,4096]{2,1,0:T(8,128)(2,1)} custom-call(bf16[16,8,4096]{2,1,0:T(8,128)(2,1)} %bitcast.102), custom_call_target="tpu_custom_call" | custom-call | tf_op jit(solution)/shard_map/exchange4/pallas_call | solution.py:297
  396.6 1.4 copy.31
  398.0 43.4 %triangle_back0.1 = bf16[16,2,8,32,128]{4,3,2,1,0:T(8,128)(2,1)S(1)} custom-call(s32[64]{0:T(128)S(1)} %reshape_squeeze.8.lists, s32[16]{0:T(128)S(1)} %get-tuple-element.54.counts, bf16[16,2,8,32,128]{4,3,2,1,0:T(8,128)(2,1)S(1)} %bitcast.86, bf16[16,8,32,128]{3,2,1,0:T(8,128)(2,1)S(1)} %copy.31), custom_call_target="tpu_custom_call" | custom-call | tf_op jit(solution)/shard_map/triangle_back0/pallas_call | solution.py:229
  441.4 1.4 copy-done.6
  442.8 4.2 reshape.125.refs_0_
  447.0 1.8 bitcast_dynamic-update-slice_fusion
  450.1 1.5 bitcast_dynamic-update-slice_fusion.2
  452.1 52.0 %exchange5.1 = (bf16[16,16,4096]{2,1,0:T(8,128)(2,1)}, bf16[16,8,1024]{2,1,0:T(8,128)(2,1)}) custom-call(bf16[16,16,4096]{2,1,0:T(8,128)(2,1)} %reshape.125.refs_0_, bf16[16,8,1024]{2,1,0:T(8,128)(2,1)} %bitcast_dynamic-update-slice_fusion.1.refs_1_), custom_call_target="tpu_custom_call" | custom-call | tf_op jit(solution)/shard_map/exchange5/pallas_call | solution.py:297
  504.2 1.6 copy-done.19
  505.8 1.2 copy-done.22
  507.0 13.1 %last.1 = (bf16[2,32,64,128]{3,2,1,0:T(8,128)(2,1)}, f32[128,512]{1,0:T(8,128)S(1)}) custom-call(bf16[2,32,64,128]{3,2,1,0:T(8,128)(2,1)S(1)} %bitcast.92, f32[128,4096]{1,0:T(8,128)S(1)} %copy-done.18, bf16[256,4096]{1,0:T(8,128)(2,1)S(1)} %bitcast.100, bf16[128,4096]{1,0:T(8,128)(2,1)S(1)} %copy-done.22, bf16[256,128]{1,0:T(8,128)(2,1)S(1)} %bitcast.107, ...), custom_call_target="tpu_custom_call" | custom-call | tf_op jit(solution)/shard_map/last/pallas_call | solution.py:151
  522.1 14.4 %exchange8.1 = bf16[16,8,512]{2,1,0:T(8,128)(2,1)} custom-call(bf16[16,8,512]{2,1,0:T(8,128)(2,1)} %convert_bitcast_fusion.refs_0_), custom_call_target="tpu_custom_call" | custom-call | tf_op jit(solution)/shard_map/exchange8/pallas_call | solution.py:297
  (84 shorter events, 17.8 us)
Async XLA Ops:
  0.6 4.0 copy-start.2
  8.8 1.4 copy-start.7
  67.1 1.0 copy-start.10
  99.9 1.2 copy-start.3
  108.0 1.0 copy-start.14
  108.9 1.4 copy-start.20
  167.6 1.4 copy-start
  169.0 1.0 copy-start.11
  202.2 1.2 copy-start.9
  203.4 1.2 copy-start.12
  204.6 1.2 copy-start.15
  214.3 1.0 copy-start.24
  215.2 1.0 copy-start.25
  216.2 0.7 copy-start.28
  216.9 0.6 copy-start.30
  244.7 1.9 copy-start.1
  285.0 1.3 copy-start.5
  337.3 1.2 copy-start.4
  338.5 1.6 copy-start.8
  340.1 1.2 copy-start.13
  341.3 1.2 copy-start.16
  342.5 1.2 copy-start.26
  361.4 1.4 copy-start.17
  362.7 1.0 copy-start.21
  363.7 1.0 copy-start.23
  364.7 0.7 copy-start.27
  365.4 0.6 copy-start.32
  366.0 0.6 copy-start.34
  441.4 1.4 copy-start.6
  442.8 6.0 %copy-start.31 = (f32[128,128]{1,0:T(8,128)S(1)}, f32[128,128]{1,0:T(8,128)}, u32[]{:S(2)}) copy-start(f32[128,128]{1,0:T(8,128)} %copy-done.30) | copy-start | bytes 196612
  442.8 6.6 %copy-start.29 = (f32[128,128]{1,0:T(8,128)S(1)}, f32[128,128]{1,0:T(8,128)}, u32[]{:S(2)}) copy-start(f32[128,128]{1,0:T(8,128)} %copy-done.28) | copy-start | bytes 196612
  442.8 8.7 %copy-start.33 = (f32[128,128]{1,0:T(8,128)S(1)}, f32[128,128]{1,0:T(8,128)}, u32[]{:S(2)}) copy-start(f32[128,128]{1,0:T(8,128)} %copy-done.32) | copy-start | bytes 196612
  447.0 57.1 %copy-start.18 = (f32[128,4096]{1,0:T(8,128)S(1)}, f32[128,4096]{1,0:T(8,128)}, u32[]{:S(2)}) copy-start(f32[128,4096]{1,0:T(8,128)} %copy-done.17) | copy-start | bytes 6291460
  504.2 1.6 copy-start.19
  505.8 1.2 copy-start.22
  507.0 13.1 %copy-start.35 = (bf16[16,8,1024]{2,1,0:T(8,128)(2,1)S(1)}, bf16[16,8,1024]{2,1,0:T(8,128)(2,1)}, u32[]{:S(2)}) copy-start(bf16[16,8,1024]{2,1,0:T(8,128)(2,1)} %get-tuple-element.38) | copy-start | bytes 786436

commit v4 on v3

--- a/solution.py
+++ b/solution.py
@@ -169,41 +169,44 @@
     return jnp.concatenate([square[:half], square[half:]], axis=1)
 
 
-def triangle_kernel(incoming, tiles, kmax, lists, counts, lr_ref, prod_ref):
+def triangle_kernel(incoming, tiles, kmax, chans, lists, counts, lr_ref, prod_ref):
     dim = 0 if incoming else 1
 
     def one(tile, _):
-        def term(slot):
+        def term(slot, chan):
             base = (tile * kmax + slot) * 2
-            left = unfold(lr_ref[lists[base], 0, 0])
-            return dot(left, unfold(lr_ref[lists[base + 1], 1, 0]), dim, dim)
-
-        total = term(0)
-        for slot in range(1, kmax):
-            total = total + jnp.where(slot < counts[tile], term(slot), 0.0)
-        prod_ref[tile, 0] = fold(total).astype(BF16)
-        return 0
-
-    lax.fori_loop(0, tiles, one, 0, unroll=8)
-
-
-def triangle_back_kernel(incoming, tiles, kmax, lists, counts, lr_ref, gprod_ref, glr_ref, total):
+            left = unfold(lr_ref[lists[base], 0, chan])
+            return dot(left, unfold(lr_ref[lists[base + 1], 1, chan]), dim, dim)
+
+        used = counts[tile]
+        for chan in range(chans):
+            total = term(0, chan)
+            for slot in range(1, kmax):
+                total = total + jnp.where(slot < used, term(slot, chan), 0.0)
+            prod_ref[tile, chan] = fold(total).astype(BF16)
+        return 0
+
+    lax.fori_loop(0, tiles, one, 0)
+
+
+def triangle_back_kernel(incoming, tiles, kmax, chans, lists, counts, lr_ref, gprod_ref, glr_ref, total):
     total[...] = jnp.zeros_like(total)
 
     def one(tile, _):
-        grad = unfold(gprod_ref[tile, 0])
         for slot in range(kmax):
 
             def add():
                 base = (tile * kmax + slot) * 2
                 x, y = lists[base], lists[base + 1]
-                left, right = unfold(lr_ref[x, 0, 0]), unfold(lr_ref[y, 1, 0])
-                if incoming:
-                    total[0, x] += dot(right, grad, 1, 1)
-                    total[1, y] += dot(left, grad, 1, 0)
-                else:
-                    total[0, x] += dot(grad, right, 1, 0)
-                    total[1, y] += dot(grad, left, 0, 0)
+                for chan in range(chans):
+                    grad = unfold(gprod_ref[tile, chan])
+                    left, right = unfold(lr_ref[x, 0, chan]), unfold(lr_ref[y, 1, chan])
+                    if incoming:
+                        total[x, 0, chan] += dot(right, grad, 1, 1)
+                        total[y, 1, chan] += dot(left, grad, 1, 0)
+                    else:
+                        total[x, 0, chan] += dot(grad, right, 1, 0)
+                        total[y, 1, chan] += dot(grad, left, 0, 0)
 
             if slot == 0:
                 add()
@@ -211,28 +214,24 @@
                 pl.when(slot < counts[tile])(add)
         return 0
 
-    lax.fori_loop(0, tiles, one, 0, unroll=4)
+    lax.fori_loop(0, tiles, one, 0)
 
     def store(tile, _):
         for which in range(2):
-            glr_ref[tile, which, 0] = fold(total[which, tile]).astype(BF16)
-        return 0
-
-    lax.fori_loop(0, tiles, store, 0, unroll=4)
+            for chan in range(chans):
+                glr_ref[tile, which, chan] = fold(total[tile, which, chan]).astype(BF16)
+        return 0
+
+    lax.fori_loop(0, tiles, store, 0)
 
 
 def tile_call(kernel, name, scalars, arrays, out_shape, scratch):
-    def spec(shape):
-        lead = len(shape) - 3
-        return pl.BlockSpec(shape[:lead] + (1,) + shape[-2:], lambda n: (0,) * lead + (n, 0, 0))
-
     return pl.pallas_call(
         kernel,
         name=name,
-        grid=(out_shape[-3],),
         in_specs=[pl.BlockSpec(memory_space=pltpu.SMEM)] * len(scalars)
-        + [spec(array.shape) for array in arrays],
-        out_specs=spec(out_shape),
+        + [pl.BlockSpec(memory_space=pltpu.VMEM)] * len(arrays),
+        out_specs=pl.BlockSpec(memory_space=pltpu.VMEM),
         out_shape=jax.ShapeDtypeStruct(out_shape, BF16),
         scratch_shapes=scratch,
         compiler_params=pltpu.CompilerParams(vmem_limit_bytes=VMEM_BYTES),
@@ -329,7 +328,7 @@
     def triangle(lr, m):
         (lr,) = exchange(2 * m, lr.reshape(devices, 2 * chans, cells))
         lr = lr.reshape(tiles, 2, chans, *folded)
-        kernel = functools.partial(triangle_kernel, m == 1, tiles, kmax)
+        kernel = functools.partial(triangle_kernel, m == 1, tiles, kmax, chans)
         prod = tile_call(kernel, f"triangle{m}", lists(m), (lr,), (tiles, chans, *folded), [])
         (prod,) = exchange(2 * m + 1, prod.reshape(tiles, chans, cells))
         return lr, prod.reshape(channels, cells)
@@ -337,8 +336,8 @@
     def triangle_back(lr, gprod, m, *others):
         (gprod,) = exchange(4 + 2 * m, gprod.reshape(devices, chans, cells))
         gprod = gprod.reshape(tiles, chans, *folded)
-        kernel = functools.partial(triangle_back_kernel, m == 1, tiles, kmax)
-        sums = pltpu.VMEM((2, tiles, side, side), F32)
+        kernel = functools.partial(triangle_back_kernel, m == 1, tiles, kmax, chans)
+        sums = pltpu.VMEM((tiles, 2, chans, side, side), F32)
         glr = tile_call(kernel, f"triangle_back{m}", lists(m), (lr, gprod), lr.shape, [sums])
         glr, *others = exchange(5 + 2 * m, glr.reshape(tiles, 2 * chans, cells), *others)
         return glr.reshape(wide, cells), *others

time: 540 us -> 480 us (0.89)
  Pallas kernels: 472 us -> 412 us
    pallas_call x4, Pallas kernels: 97.6 us -> 37.5 us  [tile_call(): pl.pallas_call(kernel, name=name, in_specs=[pl.BlockSpec(memory_space=plt...]
where the time goes in v4:
time: 480 us; the launch traced here: 479 us
  Pallas kernels  412 us (86%)
  local copies, waits for them, and re-layouts  58 us (12%)
  other arithmetic  8.56 us (2%)
    pallas_call x9, Pallas kernels, exchange(): pl.pallas_call(functools.partial(exchange_kernel, amount, devices), name=...  324 us
    pallas_call x5, Pallas kernels, cellwise(): pl.pallas_call(kernel, name=name, grid=(cells // step,), in_specs=[spec(k...  50.2 us
    unnamed x77, local copies, waits for them, and re-layouts  41 us
    pallas_call x4, Pallas kernels, tile_call(): pl.pallas_call(kernel, name=name, in_specs=[pl.BlockSpec(memory_space=plt...  37.5 us

profile of v4, /device:TPU:0, one launch (start us, length us, event | category | flops | bytes accessed | tf_op | source)
XLA Modules:
  0.0 479.2 jit_solution(10163969094890541970)
XLA Ops:
  3.4 1.1 copy.17
  4.6 4.1 first.1
  8.8 1.3 copy-done.7
  10.1 47.5 %exchange0.1 = bf16[16,16,4096]{2,1,0:T(8,128)(2,1)} custom-call(bf16[16,16,4096]{2,1,0:T(8,128)(2,1)} %bitcast.95), custom_call_target="tpu_custom_call" | custom-call | tf_op jit(solution)/shard_map/exchange0/pallas_call | solution.py:296
  57.6 2.1 copy.25
  59.7 6.9 %triangle0.1 = bf16[16,8,32,128]{3,2,1,0:T(8,128)(2,1)S(1)} custom-call(s32[64]{0:T(128)S(1)} %reshape_squeeze.8.lists, s32[16]{0:T(128)S(1)} %get-tuple-element.54.counts, bf16[16,2,8,32,128]{4,3,2,1,0:T(8,128)(2,1)S(1)} %bitcast.85), custom_call_target="tpu_custom_call" | custom-call | tf_op jit(solution)/shard_map/triangle0/pallas_call | solution.py:229
  67.6 2.3 reshape.111.refs_0_
  69.9 29.5 %exchange1.1 = bf16[16,8,4096]{2,1,0:T(8,128)(2,1)} custom-call(bf16[16,8,4096]{2,1,0:T(8,128)(2,1)} %reshape.111.refs_0_), custom_call_target="tpu_custom_call" | custom-call | tf_op jit(solution)/shard_map/exchange1/pallas_call | solution.py:296
  99.4 1.2 copy-done.3
  100.6 6.9 %middle.1 = (bf16[128,4096]{1,0:T(8,128)(2,1)S(1)}, bf16[256,4096]{1,0:T(8,128)(2,1)S(1)}) custom-call(bf16[2,32,64,128]{3,2,1,0:T(8,128)(2,1)S(1)} %bitcast.90, bf16[128,4096]{1,0:T(8,128)(2,1)S(1)} %bitcast.93, bf16[128,128]{1,0:T(8,128)(2,1)S(1)} %get-tuple-element.55.wgate.wgate0, bf16[128,128]{1,0:T(8,128)(2,1)S(1)} %get-tuple-element.44.wout.wout0, ...), custom_call_target="tpu_custom_call" | custom-call | tf_op jit(solution)/shard_map/middle/pallas_call | solution.py:151
  108.5 1.4 copy-done.20
  109.8 46.8 %exchange2.1 = bf16[16,16,4096]{2,1,0:T(8,128)(2,1)} custom-call(bf16[16,16,4096]{2,1,0:T(8,128)(2,1)} %bitcast.101), custom_call_target="tpu_custom_call" | custom-call | tf_op jit(solution)/shard_map/exchange2/pallas_call | solution.py:296
  156.6 2.1 copy.26
  158.7 8.0 %triangle1.1 = bf16[16,8,32,128]{3,2,1,0:T(8,128)(2,1)S(1)} custom-call(s32[64]{0:T(128)S(1)} %reshape_squeeze.9.lists, s32[16]{0:T(128)S(1)} %get-tuple-element.53.counts, bf16[16,2,8,32,128]{4,3,2,1,0:T(8,128)(2,1)S(1)} %bitcast.87), custom_call_target="tpu_custom_call" | custom-call | tf_op jit(solution)/shard_map/triangle1/pallas_call | solution.py:229
  166.7 1.4 copy-done
  169.0 2.3 reshape.115.refs_0_
  171.3 29.9 %exchange3.1 = bf16[16,8,4096]{2,1,0:T(8,128)(2,1)} custom-call(bf16[16,8,4096]{2,1,0:T(8,128)(2,1)} %reshape.115.refs_0_), custom_call_target="tpu_custom_call" | custom-call | tf_op jit(solution)/shard_map/exchange3/pallas_call | solution.py:296
  201.2 1.2 copy-done.9
  202.4 1.2 copy-done.12
  203.7 1.2 copy-done.15
  204.9 8.4 %top.1 = (bf16[2,32,64,128]{3,2,1,0:T(8,128)(2,1)}, bf16[128,4096]{1,0:T(8,128)(2,1)S(1)}, bf16[128,4096]{1,0:T(8,128)(2,1)S(1)}, f32[128,128]{1,0:T(8,128)S(1)}, f32[128,128]{1,0:T(8,128)S(1)}) custom-call(bf16[128,4096]{1,0:T(8,128)(2,1)S(1)} %copy-done.15, bf16[128,4096]{1,0:T(8,128)(2,1)S(1)} %bitcast.97, bf16[2,32,64,128]{3,2,1,0:T(8,128)(2,1)S(1)} %bitcast.98, ...), custom_call_target="tpu_custom_call" | custom-call | tf_op jit(solution)/shard_map/top/pallas_call | solution.py:151
  214.3 1.0 copy-done.25
  216.6 27.1 %exchange6.1 = bf16[16,8,4096]{2,1,0:T(8,128)(2,1)} custom-call(bf16[16,8,4096]{2,1,0:T(8,128)(2,1)} %bitcast.103), custom_call_target="tpu_custom_call" | custom-call | tf_op jit(solution)/shard_map/exchange6/pallas_call | solution.py:296
  243.7 1.6 copy.32
  245.6 11.1 %triangle_back1.1 = bf16[16,2,8,32,128]{4,3,2,1,0:T(8,128)(2,1)S(1)} custom-call(s32[64]{0:T(128)S(1)} %reshape_squeeze.9.lists, s32[16]{0:T(128)S(1)} %get-tuple-element.53.counts, bf16[16,2,8,32,128]{4,3,2,1,0:T(8,128)(2,1)S(1)} %bitcast.88, bf16[16,8,32,128]{3,2,1,0:T(8,128)(2,1)S(1)} %copy.32), custom_call_target="tpu_custom_call" | custom-call | tf_op jit(solution)/shard_map/triangle_back1/pallas_call | solution.py:229
  256.7 1.3 copy-done.5
  258.1 4.2 reshape.121.refs_0_
  262.2 46.8 %exchange7.1 = bf16[16,16,4096]{2,1,0:T(8,128)(2,1)} custom-call(bf16[16,16,4096]{2,1,0:T(8,128)(2,1)} %reshape.121.refs_0_), custom_call_target="tpu_custom_call" | custom-call | tf_op jit(solution)/shard_map/exchange7/pallas_call | solution.py:296
  309.0 1.2 copy-done.4
  310.2 1.6 copy-done.8
  311.8 1.2 copy-done.13
  313.1 1.2 copy-done.16
  314.3 1.2 copy-done.26
  315.5 17.6 %turn.1 = (f32[128,4096]{1,0:T(8,128)S(1)}, bf16[128,4096]{1,0:T(8,128)(2,1)S(1)}, bf16[128,4096]{1,0:T(8,128)(2,1)S(1)}, f32[128,512]{1,0:T(8,128)S(1)}, f32[12...) custom-call(bf16[128,4096]{1,0:T(8,128)(2,1)S(1)} %copy-done.16, bf16[2,32,64,128]{3,2,1,0:T(8,128)(2,1)S(1)} %bitcast.99, ...), custom_call_target="tpu_custom_call" | custom-call | tf_op jit(solution)/shard_map/turn/pallas_call | solution.py:151
  333.1 1.3 copy-done.17
  334.5 1.0 copy-done.21
  338.4 29.9 %exchange4.1 = bf16[16,8,4096]{2,1,0:T(8,128)(2,1)} custom-call(bf16[16,8,4096]{2,1,0:T(8,128)(2,1)} %bitcast.102), custom_call_target="tpu_custom_call" | custom-call | tf_op jit(solution)/shard_map/exchange4/pallas_call | solution.py:296
  368.3 1.4 copy.31
  369.8 11.5 %triangle_back0.1 = bf16[16,2,8,32,128]{4,3,2,1,0:T(8,128)(2,1)S(1)} custom-call(s32[64]{0:T(128)S(1)} %reshape_squeeze.8.lists, s32[16]{0:T(128)S(1)} %get-tuple-element.54.counts, bf16[16,2,8,32,128]{4,3,2,1,0:T(8,128)(2,1)S(1)} %bitcast.86, bf16[16,8,32,128]{3,2,1,0:T(8,128)(2,1)S(1)} %copy.31), custom_call_target="tpu_custom_call" | custom-call | tf_op jit(solution)/shard_map/triangle_back0/pallas_call | solution.py:229
  381.3 1.4 copy-done.6
  382.7 4.2 reshape.125.refs_0_
  386.9 1.8 bitcast_dynamic-update-slice_fusion
  390.0 1.5 bitcast_dynamic-update-slice_fusion.2
  392.0 52.0 %exchange5.1 = (bf16[16,16,4096]{2,1,0:T(8,128)(2,1)}, bf16[16,8,1024]{2,1,0:T(8,128)(2,1)}) custom-call(bf16[16,16,4096]{2,1,0:T(8,128)(2,1)} %reshape.125.refs_0_, bf16[16,8,1024]{2,1,0:T(8,128)(2,1)} %bitcast_dynamic-update-slice_fusion.1.refs_1_), custom_call_target="tpu_custom_call" | custom-call | tf_op jit(solution)/shard_map/exchange5/pallas_call | solution.py:296
  444.1 1.6 copy-done.19
  445.7 1.2 copy-done.22
  446.9 13.1 %last.1 = (bf16[2,32,64,128]{3,2,1,0:T(8,128)(2,1)}, f32[128,512]{1,0:T(8,128)S(1)}) custom-call(bf16[2,32,64,128]{3,2,1,0:T(8,128)(2,1)S(1)} %bitcast.92, f32[128,4096]{1,0:T(8,128)S(1)} %copy-done.18, bf16[256,4096]{1,0:T(8,128)(2,1)S(1)} %bitcast.100, bf16[128,4096]{1,0:T(8,128)(2,1)S(1)} %copy-done.22, bf16[256,128]{1,0:T(8,128)(2,1)S(1)} %bitcast.107, ...), custom_call_target="tpu_custom_call" | custom-call | tf_op jit(solution)/shard_map/last/pallas_call | solution.py:151
  462.0 14.4 %exchange8.1 = bf16[16,8,512]{2,1,0:T(8,128)(2,1)} custom-call(bf16[16,8,512]{2,1,0:T(8,128)(2,1)} %convert_bitcast_fusion.refs_0_), custom_call_target="tpu_custom_call" | custom-call | tf_op jit(solution)/shard_map/exchange8/pallas_call | solution.py:296
  (84 shorter events, 17.8 us)
Async XLA Ops:
  0.6 4.0 copy-start.2
  8.8 1.4 copy-start.7
  66.6 1.0 copy-start.10
  99.4 1.2 copy-start.3
  107.5 1.0 copy-start.14
  108.5 1.4 copy-start.20
  166.7 1.4 copy-start
  168.0 1.0 copy-start.11
  201.2 1.2 copy-start.9
  202.4 1.2 copy-start.12
  203.7 1.2 copy-start.15
  213.3 1.0 copy-start.24
  214.3 1.0 copy-start.25
  215.3 0.7 copy-start.28
  216.0 0.6 copy-start.30
  243.7 1.9 copy-start.1
  256.7 1.3 copy-start.5
  309.0 1.2 copy-start.4
  310.2 1.6 copy-start.8
  311.8 1.2 copy-start.13
  313.1 1.2 copy-start.16
  314.3 1.2 copy-start.26
  333.1 1.4 copy-start.17
  334.5 1.0 copy-start.21
  335.5 1.0 copy-start.23
  336.4 0.7 copy-start.27
  337.1 0.6 copy-start.32
  337.8 0.6 copy-start.34
  381.3 1.4 copy-start.6
  382.7 6.0 %copy-start.31 = (f32[128,128]{1,0:T(8,128)S(1)}, f32[128,128]{1,0:T(8,128)}, u32[]{:S(2)}) copy-start(f32[128,128]{1,0:T(8,128)} %copy-done.30) | copy-start | bytes 196612
  382.7 6.6 %copy-start.29 = (f32[128,128]{1,0:T(8,128)S(1)}, f32[128,128]{1,0:T(8,128)}, u32[]{:S(2)}) copy-start(f32[128,128]{1,0:T(8,128)} %copy-done.28) | copy-start | bytes 196612
  382.7 8.7 %copy-start.33 = (f32[128,128]{1,0:T(8,128)S(1)}, f32[128,128]{1,0:T(8,128)}, u32[]{:S(2)}) copy-start(f32[128,128]{1,0:T(8,128)} %copy-done.32) | copy-start | bytes 196612
  386.9 57.1 %copy-start.18 = (f32[128,4096]{1,0:T(8,128)S(1)}, f32[128,4096]{1,0:T(8,128)}, u32[]{:S(2)}) copy-start(f32[128,4096]{1,0:T(8,128)} %copy-done.17) | copy-start | bytes 6291460
  444.1 1.6 copy-start.19
  445.7 1.2 copy-start.22
  446.9 13.1 %copy-start.35 = (bf16[16,8,1024]{2,1,0:T(8,128)(2,1)S(1)}, bf16[16,8,1024]{2,1,0:T(8,128)(2,1)}, u32[]{:S(2)}) copy-start(bf16[16,8,1024]{2,1,0:T(8,128)(2,1)} %get-tuple-element.38) | copy-start | bytes 786436
